TPU v7x, 32 devices: a whole 2x2x4 slice. The times are simulated.
32 devices in a mesh: lat: 4 (over x, core), lon: 8 (over z, y).
Axes of the slice: x: 2, y: 2, z: 4, core: 2. Of those that a mesh axis runs over, the one named last changes fastest.
Arguments:
- state: bfloat16 [64, 64, 256], P('lat', 'lon'), may hold values from -45 to 45
- cotangent: bfloat16 [64, 64, 256], P('lat', 'lon'), may hold values from -6 to 6
- land_sea: int32 [64, 64], P('lat', 'lon'), may hold values 0 or 1
- regime: int32 [4, 8, 16, 8, 1], P('lat', 'lon'), may hold values from 0 to 15; in each aligned block of 128 rows (0 to 127, 128 to 255, ..., all dimensions but the last counted through in order) at most 16 rows name the same one
- first_gain: float32 [256], replicated, may hold values from 0.1 to 1.9
- second_gain: float32 [256], replicated, may hold values from 0.1 to 1.9
- project_weight: bfloat16 [256, 768], replicated, may hold values from -0.375 to 0.375
- out_weight: bfloat16 [256, 256], replicated, may hold values from -0.375 to 0.375
- pos_bias: float32 [8, 49], replicated, may hold values from -3 to 315
- up_weight: bfloat16 [256, 16384], P(None, 'lon'), may hold values from -0.375 to 0.375
- down_weight: bfloat16 [16384, 256], P('lon'), may hold values from -0.1875 to 0.1875
Outputs:
- block_out: bfloat16 [64, 64, 256], P('lat', 'lon')
- grad_up: float32 [256, 16384], P(None, 'lon')
- grad_down: float32 [16384, 256], P('lon')
Inputs may be any that keep to these rules, and one draw needn't show every extreme that they name: Among the 16 x 8 cells of one tile at most 16 share a regime, and some tile has exactly 16 cells of one regime. Every regime occurs somewhere.
All inputs are finite; a program needn't handle non-finite values. No bound on the sum of `land_sea` on one device may be relied on, other than what follows from the above.
Results may differ from a plain program's by a relative error of at most 0.022.
Values may be sent and summed in bfloat16 or wider, within the bound.
A program may use at most 64 MiB of HBM per device.

v0:
```python
import math

import jax
import jax.numpy as jnp
from jax import lax
from jax.sharding import PartitionSpec as P

WINDOW = 7
EXPERTS = 16


def from_partner(value, axis, apart):
    mask = 2**apart
    pairs = [(source, source ^ mask) for source in range(lax.axis_size(axis))]
    return lax.ppermute(value, axis, pairs)


def extended(cells, sides, width, closed):
    for axis, dim in sides:
        count = lax.axis_size(axis)
        ends = count if closed else count - 1
        head = lax.slice_in_dim(cells, 0, width, axis=dim)
        tail = lax.slice_in_dim(cells, cells.shape[dim] - width, cells.shape[dim], axis=dim)
        cells = jnp.concatenate(
            [
                lax.ppermute(tail, axis, [(i, (i + 1) % count) for i in range(ends)]),
                cells,
                lax.ppermute(head, axis, [((i + 1) % count, i) for i in range(ends)]),
            ],
            axis=dim,
        )
    return cells


def layer_norm(values, gain_vec):
    values = values.astype(jnp.float32)
    mean_val = jnp.mean(values, axis=-1, keepdims=True)
    spread = jnp.mean(jnp.square(values - mean_val), axis=-1, keepdims=True)
    return ((values - mean_val) * lax.rsqrt(spread + 1e-05) * gain_vec).astype(jnp.bfloat16)


def gelu_value(inputs):
    return 0.5 * inputs * (1.0 + jax.scipy.special.erf(inputs * 0.7071067811865476))


def gelu_slope(inputs):
    return (
        0.5 * (1.0 + jax.scipy.special.erf(inputs * 0.7071067811865476))
        + inputs * jnp.exp(-0.5 * inputs * inputs) * 0.3989422804014327
    )


def expert_pass(inputs, tangents, up_block, down_block):
    hidden = jnp.einsum("nlsd,dlf->nlsf", inputs, up_block, preferred_element_type=jnp.float32)
    active = gelu_value(hidden).astype(jnp.bfloat16)
    outputs = jnp.einsum("nlsf,lfd->nlsd", active, down_block, preferred_element_type=jnp.float32)
    back_act = jnp.einsum(
        "nlsd,lfd->nlsf", tangents, down_block, preferred_element_type=jnp.float32
    )
    pre_act = (back_act * gelu_slope(hidden)).astype(jnp.bfloat16)
    grad_down = jnp.einsum("nlsf,nlsd->lfd", active, tangents, preferred_element_type=jnp.float32)
    grad_up = jnp.einsum("nlsd,nlsf->dlf", inputs, pre_act, preferred_element_type=jnp.float32)
    return (outputs, grad_up, grad_down)


def halve(grad_u, grad_d, lon_index, group_size):
    for bit_level in reversed(range(group_size.bit_length() - 1)):
        half_units = grad_u.shape[1] // 2
        high_bit = lon_index >> bit_level & 1 == 1
        keep_u = jnp.where(high_bit, grad_u[:, half_units:], grad_u[:, :half_units])
        give_u = jnp.where(high_bit, grad_u[:, :half_units], grad_u[:, half_units:])
        keep_d = jnp.where(high_bit, grad_d[half_units:], grad_d[:half_units])
        give_d = jnp.where(high_bit, grad_d[:half_units], grad_d[half_units:])
        taken_u, taken_d = (
            from_partner(give_u.astype(jnp.bfloat16), "lon", bit_level).astype(give_u.dtype),
            from_partner(give_d.astype(jnp.bfloat16), "lon", bit_level).astype(give_d.dtype),
        )
        grad_u = keep_u + taken_u
        grad_d = keep_d + taken_d
    return (grad_u, grad_d)


def on_device(
    state,
    cotangent,
    land_sea,
    regime,
    first_gain,
    second_gain,
    project_weight,
    out_weight,
    pos_bias,
    up_weight,
    down_weight,
):
    lat_rows, lon_cols, features = state.shape
    cell_count = lat_rows * lon_cols
    head_count = pos_bias.shape[0]
    head_dim = features // head_count
    window_reach = WINDOW // 2
    tap_count = WINDOW * WINDOW
    score_scale = 1.0 / math.sqrt(head_dim)
    normed_in = layer_norm(state, first_gain)
    flat_in = normed_in.reshape(cell_count, features)
    queries = jnp.dot(
        flat_in, project_weight[:, :features], preferred_element_type=jnp.float32
    ).astype(jnp.bfloat16)
    own_kv = jnp.dot(flat_in, project_weight[:, features:], preferred_element_type=jnp.float32)
    own_kv = own_kv.astype(jnp.bfloat16).reshape(lat_rows, lon_cols, 2 * features)
    wide_kv = extended(own_kv, (("lon", 1),), window_reach, True)
    keyvals = extended(wide_kv, (("lat", 0),), window_reach, False)
    wide_mask = extended(land_sea, (("lon", 1),), window_reach, True)
    full_mask = extended(wide_mask, (("lat", 0),), window_reach, False)
    feature_first = jnp.transpose(keyvals, (2, 0, 1))
    query_heads = queries.T.reshape(head_count, head_dim, cell_count)
    score_list = []
    mask_list = []
    for row_shift in range(WINDOW):
        for col_shift in range(WINDOW):
            key_tap = feature_first[
                :features, row_shift : row_shift + lat_rows, col_shift : col_shift + lon_cols
            ].reshape(head_count, head_dim, cell_count)
            score_list.append(
                jnp.einsum("hxc,hxc->hc", query_heads, key_tap, preferred_element_type=jnp.float32)
            )
            mask_list.append(
                full_mask[
                    row_shift : row_shift + lat_rows, col_shift : col_shift + lon_cols
                ].reshape(cell_count)
            )
    scores = jnp.stack(score_list) * score_scale + pos_bias.T[:, :, None]
    tap_ids = jnp.arange(tap_count, dtype=jnp.int32)[:, None]
    valid_mask = jnp.logical_or(jnp.stack(mask_list) > 0, tap_ids == tap_count // 2)[:, None, :]
    row_top = jnp.max(jnp.where(valid_mask, scores, -jnp.inf), axis=0, keepdims=True)
    raw_weights = jnp.exp(jnp.where(valid_mask, scores - row_top, -jnp.inf))
    weights = (raw_weights / jnp.sum(raw_weights, axis=0, keepdims=True)).astype(jnp.bfloat16)
    attended = jnp.zeros((head_count, head_dim, cell_count), jnp.float32)
    for row_shift in range(WINDOW):
        for col_shift in range(WINDOW):
            tap_index = row_shift * WINDOW + col_shift
            value_tap = feature_first[
                features:, row_shift : row_shift + lat_rows, col_shift : col_shift + lon_cols
            ].reshape(head_count, head_dim, cell_count)
            attended = attended + weights[tap_index][:, None, :].astype(
                jnp.float32
            ) * value_tap.astype(jnp.float32)
    attended = attended.reshape(features, cell_count).T.astype(jnp.bfloat16)
    residual = (
        state.reshape(cell_count, features).astype(jnp.float32)
        + jnp.dot(attended, out_weight, preferred_element_type=jnp.float32)
    ).astype(jnp.bfloat16)
    second = layer_norm(residual, second_gain)
    masked = land_sea.reshape(cell_count, 1)
    tangent = cotangent.reshape(cell_count, features) * masked.astype(jnp.bfloat16)
    labels = regime.reshape(cell_count)
    capacity = cell_count // 8
    onehot = (labels[:, None] == jnp.arange(EXPERTS, dtype=jnp.int32)[None, :]).astype(jnp.int32)
    before = jnp.cumsum(onehot, axis=0) - onehot
    rank_index = jnp.sum(before * onehot, axis=1)
    slot_index = labels * capacity + rank_index
    owner_of = (
        jnp.full((EXPERTS * capacity,), cell_count, jnp.int32)
        .at[slot_index]
        .set(jnp.arange(cell_count, dtype=jnp.int32))
    )
    send_x = jnp.concatenate([second, jnp.zeros((1, features), jnp.bfloat16)])[owner_of]
    send_c = jnp.concatenate([tangent, jnp.zeros((1, features), jnp.bfloat16)])[owner_of]
    lon_count = lax.axis_size("lon")
    lon_index = lax.axis_index("lon")
    local_count = max(1, EXPERTS // lon_count)
    group_size = max(1, lon_count // EXPERTS)
    per_peer = EXPERTS * capacity // lon_count
    got_x, got_c = (
        lax.all_to_all(
            send_x.reshape(lon_count, per_peer, features),
            "lon",
            split_axis=0,
            concat_axis=0,
            tiled=True,
        ),
        lax.all_to_all(
            send_c.reshape(lon_count, per_peer, features),
            "lon",
            split_axis=0,
            concat_axis=0,
            tiled=True,
        ),
    )
    up_block = up_weight
    down_block = down_weight
    for bit_level in range(group_size.bit_length() - 1):
        other_up, other_down = from_partner((up_block, down_block), "lon", bit_level)
        high_bit = lon_index >> bit_level & 1 == 1
        up_block = jnp.where(
            high_bit,
            jnp.concatenate([other_up, up_block], axis=1),
            jnp.concatenate([up_block, other_up], axis=1),
        )
        down_block = jnp.where(
            high_bit,
            jnp.concatenate([other_down, down_block], axis=0),
            jnp.concatenate([down_block, other_down], axis=0),
        )
    unit_count = up_block.shape[1] // local_count
    outputs, grad_u, grad_d = expert_pass(
        got_x.reshape(lon_count, local_count, per_peer // local_count, features),
        got_c.reshape(lon_count, local_count, per_peer // local_count, features),
        up_block.reshape(features, local_count, unit_count),
        down_block.reshape(local_count, unit_count, features),
    )
    returned = lax.all_to_all(
        outputs.astype(jnp.bfloat16).reshape(lon_count, per_peer, features),
        "lon",
        split_axis=0,
        concat_axis=0,
        tiled=True,
    )
    expert_rows = returned.reshape(EXPERTS * capacity, features)
    grad_u = grad_u.reshape(features, local_count * unit_count)
    grad_d = grad_d.reshape(local_count * unit_count, features)
    grad_u, grad_d = (
        lax.psum(grad_u.astype(jnp.bfloat16), "lat").astype(jnp.float32),
        lax.psum(grad_d.astype(jnp.bfloat16), "lat").astype(jnp.float32),
    )
    grad_u, grad_d = halve(grad_u, grad_d, lon_index, group_size)
    expert_cell = expert_rows[slot_index]
    result_block = (
        masked.astype(jnp.float32)
        * (residual.astype(jnp.float32) + expert_cell.astype(jnp.float32))
    ).astype(jnp.bfloat16)
    return (result_block.reshape(lat_rows, lon_cols, features), grad_u, grad_d)


def solution(mesh):
    placed = (
        P("lat", "lon", None),
        P("lat", "lon", None),
        P("lat", "lon"),
        P("lat", "lon", None, None, None),
        P(),
        P(),
        P(),
        P(),
        P(),
        P(None, "lon"),
        P("lon", None),
    )
    return jax.shard_map(
        on_device,
        mesh=mesh,
        in_specs=placed,
        out_specs=(P("lat", "lon", None), P(None, "lon"), P("lon", None)),
        check_vma=False,
    )
```

profile of v0, /device:TPU:0, one launch (start us, length us, event | category | flops | bytes accessed | tf_op | source)
XLA Modules:
  0.0 353.4 jit_solution(12095631964109723148)
XLA Ops:
  10.6 6.1 %collective-permute-start.5 = (bf16[16,3,512]{2,1,0:T(4,128)(2,1)S(1)}, bf16[16,3,512]{2,1,0:T(4,128)(2,1)S(1)}, u32[]{:S(2)}, u32[]{:S(2)}) collective-permute-start(bf16[16,3,512]{2,1,0:T(4,128)(2,1)S(1)} %get-tuple-element.155), channel_id=1, source_target_pairs={{1,0},{2,1},{3,2},{4,3},{5,4},{6,5},{7,6},{0,7},{9,8},{10,9},{11,1... | collective-permute-start | bytes 147464 | tf_op jit(solution)/shard_map/ppermute | solution.py:28
  17.4 4.7 %collective-permute-start.1 = (s32[16,3]{0,1:T(4,128)S(1)}, s32[16,3]{0,1:T(4,128)S(1)}, u32[]{:S(2)}, u32[]{:S(2)}) collective-permute-start(s32[16,3]{0,1:T(4,128)S(1)} %get-tuple-element.261), channel_id=1, source_target_pairs={{1,0},{2,1},{3,2},{4,3},{5,4},{6,5},{7,6},{0,7},{9,8},{10,9},{11,1... | collective-permute-start | bytes 584 | tf_op jit(solution)/shard_map/ppermute | solution.py:28
  30.4 3.0 collective-permute-start.2
  43.8 3.8 %collective-permute-start.6 = (bf16[3,14,512]{2,1,0:T(8,128)(2,1)S(1)}, bf16[3,14,512]{2,1,0:T(8,128)(2,1)S(1)}, u32[]{:S(2)}, u32[]{:S(2)}) collective-permute-start(bf16[3,14,512]{2,1,0:T(8,128)(2,1)S(1)} %get-tuple-element.152), channel_id=1, source_target_pairs={{0,8},{8,16},{16,24},{1,9},{9,17},{17,25},{2,10},{10,18},{18,26},{... | collective-permute-start | bytes 129032 | tf_op jit(solution)/shard_map/ppermute | solution.py:26
  57.5 1.8 reshape.1380
  59.2 1.7 reshape.1379
  61.0 1.7 reshape.1378
  62.7 1.7 reshape.1377
  64.5 1.7 reshape.1376
  66.2 1.8 reshape.1375
  68.0 4.1 %multiply_reduce_fusion.36 = (f32[8,128]{0,1:T(8,128)}, f32[8,128]{0,1:T(8,128)}, f32[8,128]{0,1:T(8,128)}, f32[8,128]{0,1:T(8,128)}, f32[8,128]{0,1:T(8,128)}, ...) fusion(f32[8,128,32]{2,0,1:T(8,128)S(1)} %copy.296, ...), kind=kLoop, calls=%fused_computation.64 | loop fusion | flops 1264640 | bytes 1036288
  73.0 1.5 copy.304
  76.0 1.5 copy.318
  77.5 1.5 copy.325
  82.0 1.5 copy.346
  83.5 1.5 copy.353
  86.5 1.5 copy.367
  88.9 1.5 copy.381
  95.9 1.7 reshape.1399
  97.6 1.7 reshape.1398
  99.4 1.7 reshape.1397
  101.1 1.7 reshape.1396
  102.8 1.7 reshape.1395
  104.6 1.8 reshape.1394
  106.3 1.8 reshape.1393
  108.1 1.8 reshape.1392
  109.9 1.7 reshape.1391
  111.6 1.8 reshape.1390
  113.4 1.8 reshape.1389
  115.1 1.7 reshape.1388
  116.9 5.5 %multiply_reduce_fusion.18 = (f32[8,128]{0,1:T(8,128)}, f32[8,128]{0,1:T(8,128)}, f32[8,128]{0,1:T(8,128)}, f32[8,128]{0,1:T(8,128)}, f32[8,128]{0,1:T(8,128)}, ...) fusion(f32[8,128,32]{2,0,1:T(8,128)S(1)} %copy.296, ...), kind=kLoop, calls=%fused_computation.46 | loop fusion | flops 1751040 | bytes 1384448
  122.4 1.5 copy.388
  126.9 1.5 copy.409
  131.4 1.5 copy.430
  135.9 1.5 copy.451
  137.4 1.5 copy.458
  146.3 1.5 copy.500
  153.9 1.7 reshape.1417
  155.6 1.9 reshape.1416
  157.6 1.7 reshape.1415
  159.3 1.7 reshape.1414
  161.1 1.7 reshape.1413
  162.8 1.8 reshape.1412
  164.6 1.8 reshape.1411
  166.3 1.8 reshape.1410
  168.1 1.7 reshape.1409
  169.9 1.8 reshape.1408
  171.6 1.8 reshape.1407
  173.4 1.7 reshape.1406
  175.1 5.4 %multiply_reduce_fusion = (f32[8,128]{0,1:T(8,128)}, f32[8,128]{0,1:T(8,128)}, f32[8,128]{0,1:T(8,128)}, f32[8,128]{0,1:T(8,128)}, f32[8,128]{0,1:T(8,128)}, /*i...) fusion(f32[8,128,32]{2,0,1:T(8,128)S(1)} %copy.296, ...), kind=kLoop, calls=%fused_computation.28 | loop fusion | flops 1751040 | bytes 1384448
  227.1 1.7 copy.272
  255.2 3.1 fusion.25
  259.0 1.8 gather_fusion
  260.8 6.0 %all-to-all-start = ((bf16[8,32,256]{2,1,0:T(8,128)(2,1)}), bf16[8,32,256]{2,1,0:T(8,128)(2,1)S(1)}, u32[]{:S(2)}, u32[]{:S(2)}) async-start(bf16[8,32,256]{2,1,0:T(8,128)(2,1)} %bitcast.401), calls=%async_computation | async-start | bytes 262144 | tf_op jit(solution)/shard_map/all_to_all | solution.py:174
  266.8 1.8 reshape.1426
  268.9 1.8 gather_fusion.2
  270.7 3.5 all-to-all-done
  274.2 3.4 all-to-all-start.2
  279.4 6.3 %all-to-all-done.2 = bf16[8,32,256]{2,1,0:T(8,128)(2,1)S(1)} async-done(((bf16[8,32,256]{2,1,0:T(8,128)(2,1)}), bf16[8,32,256]{2,1,0:T(8,128)(2,1)S(1)}, u32[]{:S(2)}, u32[]{:S(2)}) %all-to-all-start.2) | async-done | bytes 131104 | tf_op jit(solution)/shard_map/all_to_all | solution.py:181
  285.7 2.3 bitcast_convert_fusion.1
  291.9 3.4 all-to-all-start.1
  295.5 7.1 %all-to-all-done.1 = bf16[8,32,256]{2,1,0:T(8,128)(2,1)S(1)} async-done(((bf16[8,32,256]{2,1,0:T(8,128)(2,1)}), bf16[8,32,256]{2,1,0:T(8,128)(2,1)S(1)}, u32[]{:S(2)}, u32[]{:S(2)}) %all-to-all-start.1) | async-done | bytes 131104 | tf_op jit(solution)/shard_map/all_to_all | solution.py:211
  304.1 38.1 %all-reduce.5.cloned.1.call-done = (bf16[256,2048]{1,0:T(8,128)(2,1)}, bf16[2048,256]{1,0:T(8,128)(2,1)}) async-done(((bf16[256,2048]{1,0:T(8,128)(2,1)}, bf16[2048,256]{1,0:T(8,128)(2,1)}), (bf16[256,2048]{1,0:T(8,128)(2,1)}, bf16[2048,256]{1,0:T(8,128)(2,1)})) %all-reduce.5.cloned.1.call-update) | async-done | bytes 2097168 | tf_op jit(solution)/shard_map/psum | solution.py:222
  342.2 2.9 convert_element_type.1207
  (483 shorter events, 149.9 us)
Async XLA Ops:
  7.2 278.6 %copy-start = (bf16[2048,256]{1,0:T(8,128)(2,1)S(1)}, bf16[2048,256]{1,0:T(8,128)(2,1)}, u32[]{:S(2)}) copy-start(bf16[2048,256]{1,0:T(8,128)(2,1)} %param.21) | copy-start | bytes 3145732
  7.2 21.8 %copy-start.66 = (s32[16,8]{0,1:T(8,128)S(1)}, s32[16,8]{0,1:T(8,128)}, u32[]{:S(2)}) copy-start(s32[16,8]{0,1:T(8,128)} %param.13) | copy-start | bytes 1540
  7.2 21.0 %copy-start.70 = (f32[8,49]{1,0:T(8,128)S(1)}, f32[8,49]{1,0:T(8,128)}, u32[]{:S(2)}) copy-start(f32[8,49]{1,0:T(8,128)} %param.19) | copy-start | bytes 4708
  10.6 31.9 %collective-permute-start.5 = (bf16[16,3,512]{2,1,0:T(4,128)(2,1)S(1)}, bf16[16,3,512]{2,1,0:T(4,128)(2,1)S(1)}, u32[]{:S(2)}, u32[]{:S(2)}) collective-permute-start(bf16[16,3,512]{2,1,0:T(4,128)(2,1)S(1)} %get-tuple-element.155), channel_id=1, source_target_pairs={{1,0},{2,1},{3,2},{4,3},{5,4},{6,5},{7,6},{0,7},{9,8},{10,9},{11,1... | collective-permute-start | bytes 147464 | tf_op jit(solution)/shard_map/ppermute | solution.py:28
  16.6 25.8 %collective-permute-start.4 = (bf16[16,3,512]{2,1,0:T(4,128)(2,1)S(1)}, bf16[16,3,512]{2,1,0:T(4,128)(2,1)S(1)}, u32[]{:S(2)}, u32[]{:S(2)}) collective-permute-start(bf16[16,3,512]{2,1,0:T(4,128)(2,1)S(1)} %get-tuple-element.154), channel_id=1, source_target_pairs={{0,1},{1,2},{2,3},{3,4},{4,5},{5,6},{6,7},{7,0},{8,9},{9,10},{10,1... | collective-permute-start | bytes 147464 | tf_op jit(solution)/shard_map/ppermute | solution.py:26
  17.4 11.6 %collective-permute-start.1 = (s32[16,3]{0,1:T(4,128)S(1)}, s32[16,3]{0,1:T(4,128)S(1)}, u32[]{:S(2)}, u32[]{:S(2)}) collective-permute-start(s32[16,3]{0,1:T(4,128)S(1)} %get-tuple-element.261), channel_id=1, source_target_pairs={{1,0},{2,1},{3,2},{4,3},{5,4},{6,5},{7,6},{0,7},{9,8},{10,9},{11,1... | collective-permute-start | bytes 584 | tf_op jit(solution)/shard_map/ppermute | solution.py:28
  22.1 6.8 %collective-permute-start = (s32[16,3]{0,1:T(4,128)S(1)}, s32[16,3]{0,1:T(4,128)S(1)}, u32[]{:S(2)}, u32[]{:S(2)}) collective-permute-start(s32[16,3]{0,1:T(4,128)S(1)} %get-tuple-element.260), channel_id=1, source_target_pairs={{0,1},{1,2},{2,3},{3,4},{4,5},{5,6},{6,7},{7,0},{8,9},{9,10},{10,1... | collective-permute-start | bytes 584 | tf_op jit(solution)/shard_map/ppermute | solution.py:26
  29.1 5.9 %collective-permute-start.3 = (s32[3,14]{0,1:T(8,128)S(1)}, s32[3,14]{0,1:T(8,128)S(1)}, u32[]{:S(2)}, u32[]{:S(2)}) collective-permute-start(s32[3,14]{0,1:T(8,128)S(1)} %get-tuple-element.228), channel_id=1, source_target_pairs={{8,0},{16,8},{24,16},{9,1},{17,9},{25,17},{10,2},{18,10},{26,18},{... | collective-permute-start | bytes 512 | tf_op jit(solution)/shard_map/ppermute | solution.py:28
  30.4 4.6 %collective-permute-start.2 = (s32[3,14]{0,1:T(8,128)S(1)}, s32[3,14]{0,1:T(8,128)S(1)}, u32[]{:S(2)}, u32[]{:S(2)}) collective-permute-start(s32[3,14]{0,1:T(8,128)S(1)} %get-tuple-element.229), channel_id=1, source_target_pairs={{0,8},{8,16},{16,24},{1,9},{9,17},{17,25},{2,10},{10,18},{18,26},{... | collective-permute-start | bytes 512 | tf_op jit(solution)/shard_map/ppermute | solution.py:26
  42.5 5.2 %collective-permute-start.7 = (bf16[3,14,512]{2,1,0:T(8,128)(2,1)S(1)}, bf16[3,14,512]{2,1,0:T(8,128)(2,1)S(1)}, u32[]{:S(2)}, u32[]{:S(2)}) collective-permute-start(bf16[3,14,512]{2,1,0:T(8,128)(2,1)S(1)} %get-tuple-element.153), channel_id=1, source_target_pairs={{8,0},{16,8},{24,16},{9,1},{17,9},{25,17},{10,2},{18,10},{26,18},{... | collective-permute-start | bytes 129032 | tf_op jit(solution)/shard_map/ppermute | solution.py:28
  43.8 4.5 %collective-permute-start.6 = (bf16[3,14,512]{2,1,0:T(8,128)(2,1)S(1)}, bf16[3,14,512]{2,1,0:T(8,128)(2,1)S(1)}, u32[]{:S(2)}, u32[]{:S(2)}) collective-permute-start(bf16[3,14,512]{2,1,0:T(8,128)(2,1)S(1)} %get-tuple-element.152), channel_id=1, source_target_pairs={{0,8},{8,16},{16,24},{1,9},{9,17},{17,25},{2,10},{10,18},{18,26},{... | collective-permute-start | bytes 129032 | tf_op jit(solution)/shard_map/ppermute | solution.py:26
  72.1 22.5 %copy-start.64 = (bf16[256,16,8]{0,2,1:T(8,128)(2,1)S(1)}, bf16[256,16,8]{0,2,1:T(8,128)(2,1)}, u32[]{:S(2)}) copy-start(bf16[256,16,8]{0,2,1:T(8,128)(2,1)} %get-tuple-element.125) | copy-start | bytes 196612
  122.4 30.1 %copy-start.63 = (bf16[256,16,8]{0,2,1:T(8,128)(2,1)S(1)}, bf16[256,16,8]{0,2,1:T(8,128)(2,1)}, u32[]{:S(2)}) copy-start(bf16[256,16,8]{0,2,1:T(8,128)(2,1)} %get-tuple-element.109) | copy-start | bytes 196612
  122.4 30.3 %copy-start.62 = (bf16[256,16,8]{0,2,1:T(8,128)(2,1)S(1)}, bf16[256,16,8]{0,2,1:T(8,128)(2,1)}, u32[]{:S(2)}) copy-start(bf16[256,16,8]{0,2,1:T(8,128)(2,1)} %get-tuple-element.110) | copy-start | bytes 196612
  180.6 38.3 %copy-start.61 = (f32[49,8]{1,0:T(8,128)S(1)}, f32[49,8]{1,0:T(8,128)}, u32[]{:S(2)}) copy-start(f32[49,8]{1,0:T(8,128)} %copy.231) | copy-start | bytes 4708
  180.6 40.4 %copy-start.49 = (f32[256,128]{0,1:T(8,128)S(1)}, f32[256,128]{0,1:T(8,128)}, u32[]{:S(2)}) copy-start(f32[256,128]{0,1:T(8,128)} %get-tuple-element.55) | copy-start | bytes 393220
  180.6 41.2 %copy-start.48 = (f32[256,128]{0,1:T(8,128)S(1)}, f32[256,128]{0,1:T(8,128)}, u32[]{:S(2)}) copy-start(f32[256,128]{0,1:T(8,128)} %get-tuple-element.56) | copy-start | bytes 393220
  180.6 42.0 %copy-start.47 = (f32[256,128]{0,1:T(8,128)S(1)}, f32[256,128]{0,1:T(8,128)}, u32[]{:S(2)}) copy-start(f32[256,128]{0,1:T(8,128)} %get-tuple-element.57) | copy-start | bytes 393220
  180.6 42.7 %copy-start.46 = (f32[256,128]{0,1:T(8,128)S(1)}, f32[256,128]{0,1:T(8,128)}, u32[]{:S(2)}) copy-start(f32[256,128]{0,1:T(8,128)} %get-tuple-element.58) | copy-start | bytes 393220
  180.6 43.5 %copy-start.45 = (f32[256,128]{0,1:T(8,128)S(1)}, f32[256,128]{0,1:T(8,128)}, u32[]{:S(2)}) copy-start(f32[256,128]{0,1:T(8,128)} %get-tuple-element.59) | copy-start | bytes 393220
  180.6 44.2 %copy-start.44 = (f32[256,128]{0,1:T(8,128)S(1)}, f32[256,128]{0,1:T(8,128)}, u32[]{:S(2)}) copy-start(f32[256,128]{0,1:T(8,128)} %get-tuple-element.60) | copy-start | bytes 393220
  183.4 42.2 %copy-start.43 = (f32[256,128]{0,1:T(8,128)S(1)}, f32[256,128]{0,1:T(8,128)}, u32[]{:S(2)}) copy-start(f32[256,128]{0,1:T(8,128)} %get-tuple-element.61) | copy-start | bytes 393220
  187.0 39.3 %copy-start.42 = (f32[256,128]{0,1:T(8,128)S(1)}, f32[256,128]{0,1:T(8,128)}, u32[]{:S(2)}) copy-start(f32[256,128]{0,1:T(8,128)} %get-tuple-element.62) | copy-start | bytes 393220
  193.4 35.3 %copy-start.41 = (f32[256,128]{0,1:T(8,128)S(1)}, f32[256,128]{0,1:T(8,128)}, u32[]{:S(2)}) copy-start(f32[256,128]{0,1:T(8,128)} %get-tuple-element.64) | copy-start | bytes 393220
  197.1 32.4 %copy-start.40 = (f32[256,128]{0,1:T(8,128)S(1)}, f32[256,128]{0,1:T(8,128)}, u32[]{:S(2)}) copy-start(f32[256,128]{0,1:T(8,128)} %get-tuple-element.65) | copy-start | bytes 393220
  216.2 14.1 %copy-start.39 = (f32[256,128]{0,1:T(8,128)S(1)}, f32[256,128]{0,1:T(8,128)}, u32[]{:S(2)}) copy-start(f32[256,128]{0,1:T(8,128)} %get-tuple-element.66) | copy-start | bytes 393220
  217.0 14.0 %copy-start.38 = (f32[256,128]{0,1:T(8,128)S(1)}, f32[256,128]{0,1:T(8,128)}, u32[]{:S(2)}) copy-start(f32[256,128]{0,1:T(8,128)} %get-tuple-element.67) | copy-start | bytes 393220
  218.8 12.9 %copy-start.37 = (f32[256,128]{0,1:T(8,128)S(1)}, f32[256,128]{0,1:T(8,128)}, u32[]{:S(2)}) copy-start(f32[256,128]{0,1:T(8,128)} %get-tuple-element.68) | copy-start | bytes 393220
  218.9 13.7 %copy-start.36 = (f32[256,128]{0,1:T(8,128)S(1)}, f32[256,128]{0,1:T(8,128)}, u32[]{:S(2)}) copy-start(f32[256,128]{0,1:T(8,128)} %get-tuple-element.69) | copy-start | bytes 393220
  219.7 13.6 %copy-start.35 = (f32[256,128]{0,1:T(8,128)S(1)}, f32[256,128]{0,1:T(8,128)}, u32[]{:S(2)}) copy-start(f32[256,128]{0,1:T(8,128)} %get-tuple-element.70) | copy-start | bytes 393220
  221.0 13.0 %copy-start.34 = (f32[256,128]{0,1:T(8,128)S(1)}, f32[256,128]{0,1:T(8,128)}, u32[]{:S(2)}) copy-start(f32[256,128]{0,1:T(8,128)} %get-tuple-element.71) | copy-start | bytes 393220
  221.8 13.0 %copy-start.32 = (f32[256,128]{0,1:T(8,128)S(1)}, f32[256,128]{0,1:T(8,128)}, u32[]{:S(2)}) copy-start(f32[256,128]{0,1:T(8,128)} %get-tuple-element.72) | copy-start | bytes 393220
  222.5 13.0 %copy-start.33 = (f32[256,128]{0,1:T(8,128)S(1)}, f32[256,128]{0,1:T(8,128)}, u32[]{:S(2)}) copy-start(f32[256,128]{0,1:T(8,128)} %get-tuple-element.74) | copy-start | bytes 393220
  223.3 13.0 %copy-start.31 = (f32[256,128]{0,1:T(8,128)S(1)}, f32[256,128]{0,1:T(8,128)}, u32[]{:S(2)}) copy-start(f32[256,128]{0,1:T(8,128)} %get-tuple-element.75) | copy-start | bytes 393220
  224.1 13.0 %copy-start.30 = (f32[256,128]{0,1:T(8,128)S(1)}, f32[256,128]{0,1:T(8,128)}, u32[]{:S(2)}) copy-start(f32[256,128]{0,1:T(8,128)} %get-tuple-element.76) | copy-start | bytes 393220
  224.8 13.0 %copy-start.29 = (f32[256,128]{0,1:T(8,128)S(1)}, f32[256,128]{0,1:T(8,128)}, u32[]{:S(2)}) copy-start(f32[256,128]{0,1:T(8,128)} %get-tuple-element.77) | copy-start | bytes 393220
  225.6 13.0 %copy-start.28 = (f32[256,128]{0,1:T(8,128)S(1)}, f32[256,128]{0,1:T(8,128)}, u32[]{:S(2)}) copy-start(f32[256,128]{0,1:T(8,128)} %get-tuple-element.78) | copy-start | bytes 393220
  226.3 13.0 %copy-start.27 = (f32[256,128]{0,1:T(8,128)S(1)}, f32[256,128]{0,1:T(8,128)}, u32[]{:S(2)}) copy-start(f32[256,128]{0,1:T(8,128)} %get-tuple-element.79) | copy-start | bytes 393220
  227.1 13.0 %copy-start.26 = (f32[256,128]{0,1:T(8,128)S(1)}, f32[256,128]{0,1:T(8,128)}, u32[]{:S(2)}) copy-start(f32[256,128]{0,1:T(8,128)} %get-tuple-element.80) | copy-start | bytes 393220
  228.7 12.1 %copy-start.25 = (f32[256,128]{0,1:T(8,128)S(1)}, f32[256,128]{0,1:T(8,128)}, u32[]{:S(2)}) copy-start(f32[256,128]{0,1:T(8,128)} %get-tuple-element.81) | copy-start | bytes 393220
  229.5 12.1 %copy-start.24 = (f32[256,128]{0,1:T(8,128)S(1)}, f32[256,128]{0,1:T(8,128)}, u32[]{:S(2)}) copy-start(f32[256,128]{0,1:T(8,128)} %get-tuple-element.82) | copy-start | bytes 393220
  230.3 12.1 %copy-start.23 = (f32[256,128]{0,1:T(8,128)S(1)}, f32[256,128]{0,1:T(8,128)}, u32[]{:S(2)}) copy-start(f32[256,128]{0,1:T(8,128)} %get-tuple-element.83) | copy-start | bytes 393220
  231.0 12.1 %copy-start.22 = (f32[256,128]{0,1:T(8,128)S(1)}, f32[256,128]{0,1:T(8,128)}, u32[]{:S(2)}) copy-start(f32[256,128]{0,1:T(8,128)} %get-tuple-element.84) | copy-start | bytes 393220
  231.8 12.1 %copy-start.21 = (f32[256,128]{0,1:T(8,128)S(1)}, f32[256,128]{0,1:T(8,128)}, u32[]{:S(2)}) copy-start(f32[256,128]{0,1:T(8,128)} %get-tuple-element.85) | copy-start | bytes 393220
  232.5 12.1 %copy-start.19 = (f32[256,128]{0,1:T(8,128)S(1)}, f32[256,128]{0,1:T(8,128)}, u32[]{:S(2)}) copy-start(f32[256,128]{0,1:T(8,128)} %get-tuple-element.86) | copy-start | bytes 393220
  233.3 12.1 %copy-start.17 = (f32[256,128]{0,1:T(8,128)S(1)}, f32[256,128]{0,1:T(8,128)}, u32[]{:S(2)}) copy-start(f32[256,128]{0,1:T(8,128)} %get-tuple-element.87) | copy-start | bytes 393220
  234.0 12.1 %copy-start.15 = (f32[256,128]{0,1:T(8,128)S(1)}, f32[256,128]{0,1:T(8,128)}, u32[]{:S(2)}) copy-start(f32[256,128]{0,1:T(8,128)} %get-tuple-element.88) | copy-start | bytes 393220
  234.8 12.1 %copy-start.13 = (f32[256,128]{0,1:T(8,128)S(1)}, f32[256,128]{0,1:T(8,128)}, u32[]{:S(2)}) copy-start(f32[256,128]{0,1:T(8,128)} %get-tuple-element.89) | copy-start | bytes 393220
  235.5 12.1 %copy-start.11 = (f32[256,128]{0,1:T(8,128)S(1)}, f32[256,128]{0,1:T(8,128)}, u32[]{:S(2)}) copy-start(f32[256,128]{0,1:T(8,128)} %get-tuple-element.90) | copy-start | bytes 393220
  236.3 12.1 %copy-start.9 = (f32[256,128]{0,1:T(8,128)S(1)}, f32[256,128]{0,1:T(8,128)}, u32[]{:S(2)}) copy-start(f32[256,128]{0,1:T(8,128)} %get-tuple-element.91) | copy-start | bytes 393220
  237.0 12.1 %copy-start.20 = (f32[256,128]{0,1:T(8,128)S(1)}, f32[256,128]{0,1:T(8,128)}, u32[]{:S(2)}) copy-start(f32[256,128]{0,1:T(8,128)} %get-tuple-element.93) | copy-start | bytes 393220
  237.8 12.1 %copy-start.18 = (f32[256,128]{0,1:T(8,128)S(1)}, f32[256,128]{0,1:T(8,128)}, u32[]{:S(2)}) copy-start(f32[256,128]{0,1:T(8,128)} %get-tuple-element.94) | copy-start | bytes 393220
  238.6 12.1 %copy-start.16 = (f32[256,128]{0,1:T(8,128)S(1)}, f32[256,128]{0,1:T(8,128)}, u32[]{:S(2)}) copy-start(f32[256,128]{0,1:T(8,128)} %get-tuple-element.95) | copy-start | bytes 393220
  239.3 12.1 %copy-start.14 = (f32[256,128]{0,1:T(8,128)S(1)}, f32[256,128]{0,1:T(8,128)}, u32[]{:S(2)}) copy-start(f32[256,128]{0,1:T(8,128)} %get-tuple-element.96) | copy-start | bytes 393220
  240.1 12.1 %copy-start.12 = (f32[256,128]{0,1:T(8,128)S(1)}, f32[256,128]{0,1:T(8,128)}, u32[]{:S(2)}) copy-start(f32[256,128]{0,1:T(8,128)} %get-tuple-element.97) | copy-start | bytes 393220
  240.8 12.1 %copy-start.10 = (f32[256,128]{0,1:T(8,128)S(1)}, f32[256,128]{0,1:T(8,128)}, u32[]{:S(2)}) copy-start(f32[256,128]{0,1:T(8,128)} %get-tuple-element.98) | copy-start | bytes 393220
  241.6 12.0 %copy-start.8 = (f32[256,128]{0,1:T(8,128)S(1)}, f32[256,128]{0,1:T(8,128)}, u32[]{:S(2)}) copy-start(f32[256,128]{0,1:T(8,128)} %get-tuple-element.99) | copy-start | bytes 393220
  242.4 11.4 %copy-start.7 = (f32[256,128]{0,1:T(8,128)S(1)}, f32[256,128]{0,1:T(8,128)}, u32[]{:S(2)}) copy-start(f32[256,128]{0,1:T(8,128)} %get-tuple-element.100) | copy-start | bytes 393220
  243.1 10.7 %copy-start.6 = (f32[256,128]{0,1:T(8,128)S(1)}, f32[256,128]{0,1:T(8,128)}, u32[]{:S(2)}) copy-start(f32[256,128]{0,1:T(8,128)} %get-tuple-element.101) | copy-start | bytes 393220
  258.6 10.2 %copy-start.67 = (bf16[16,8,256]{2,1,0:T(8,128)(2,1)S(1)}, bf16[16,8,256]{2,1,0:T(8,128)(2,1)}, u32[]{:S(2)}) copy-start(bf16[16,8,256]{2,1,0:T(8,128)(2,1)} %param.12) | copy-start | bytes 196612
  260.8 13.5 %all-to-all-start = ((bf16[8,32,256]{2,1,0:T(8,128)(2,1)}), bf16[8,32,256]{2,1,0:T(8,128)(2,1)S(1)}, u32[]{:S(2)}, u32[]{:S(2)}) async-start(bf16[8,32,256]{2,1,0:T(8,128)(2,1)} %bitcast.401), calls=%async_computation | async-start | bytes 262144 | tf_op jit(solution)/shard_map/all_to_all | solution.py:174
  274.2 11.5 %all-to-all-start.2 = ((bf16[8,32,256]{2,1,0:T(8,128)(2,1)}), bf16[8,32,256]{2,1,0:T(8,128)(2,1)S(1)}, u32[]{:S(2)}, u32[]{:S(2)}) async-start(bf16[8,32,256]{2,1,0:T(8,128)(2,1)} %bitcast.413), calls=%async_computation.2 | async-start | bytes 262144 | tf_op jit(solution)/shard_map/all_to_all | solution.py:181
  277.6 64.6 %all-reduce.5.cloned.1.call-start = ((), (), s32[]{:S(2)}) async-start(), calls=%async_computation.3 | async-start | bytes 4194304 | tf_op jit(solution)/shard_map/psum | solution.py:222
  291.9 10.7 %all-to-all-start.1 = ((bf16[8,32,256]{2,1,0:T(8,128)(2,1)}), bf16[8,32,256]{2,1,0:T(8,128)(2,1)S(1)}, u32[]{:S(2)}, u32[]{:S(2)}) async-start(bf16[8,32,256]{2,1,0:T(8,128)(2,1)} %bitcast.409), calls=%async_computation.1 | async-start | bytes 262144 | tf_op jit(solution)/shard_map/all_to_all | solution.py:211
  (22 other events, 131.0 us)
Sparse Core Ops, SparseCore 0:
  291.0 51.1 all-reduce.4
where the time goes:
time: 359 us; the launch traced here: 353 us
  local copies, waits for them, and re-layouts  205 us (57%)
  waiting for transfers between devices  55.7 us (16%)
  other arithmetic  36.4 us (10%)
  starting transfers between devices  33.3 us (9%)
  between operations  15.4 us (4%)
  matrix products  8.19 us (2%)
    reshape x49, local copies, waits for them, and re-layouts, on_device(): key_tap = feature_first[:features, row_shift:row_shift + lat_rows, col_sh...  64.6 us
    dot_general x49, local copies, waits for them, and re-layouts, on_device(): jnp.einsum('hxc,hxc->hc', query_heads, key_tap, preferred_element_type=jn...  61.8 us
    psum x1, waiting for transfers between devices, on_device(): lax.psum(grad_u.astype(jnp.bfloat16), 'lat').astype(jnp.float32)  38.1 us
    convert_element_type x49, local copies, waits for them, and re-layouts, on_device(): value_tap.astype(jnp.float32)  33.7 us
    unnamed x200, local copies, waits for them, and re-layouts  21.9 us
    unnamed x3, other arithmetic  15 us
    ppermute x4, starting transfers between devices, extended(): lax.ppermute(head, axis, [((i + 1) % count, i) for i in range(ends)])  13.4 us
  transfers between devices with their start and end apart: 12, of which 5 were waited for; matrix products, arithmetic and copies ran while one was open for 7% of the time, Pallas kernels for 0%

commit v1 on v0

--- a/solution.py
+++ b/solution.py
@@ -1,8 +1,11 @@
+import functools
 import math
 
 import jax
 import jax.numpy as jnp
 from jax import lax
+from jax.experimental import pallas as pl
+from jax.experimental.pallas import tpu as pltpu
 from jax.sharding import PartitionSpec as P
 
 WINDOW = 7
@@ -80,7 +83,7 @@
     return (grad_u, grad_d)
 
 
-def on_device(
+def on_device_general(
     state,
     cotangent,
     land_sea,
@@ -231,6 +234,417 @@
     return (result_block.reshape(lat_rows, lon_cols, features), grad_u, grad_d)
 
 
+MESH = pl.DeviceIdType.MESH
+HALO = 32
+LANES = 128
+
+
+def dot(left, right, dims=((1,), (0,))):
+    return lax.dot_general(left, right, (dims, ((), ())), preferred_element_type=jnp.float32)
+
+
+def norm_rows(values, gain_row):
+    mean_val = jnp.mean(values, axis=-1, keepdims=True)
+    centred = values - mean_val
+    spread = jnp.mean(jnp.square(centred), axis=-1, keepdims=True)
+    return (centred * lax.rsqrt(spread + 1e-05) * gain_row).astype(jnp.bfloat16)
+
+
+def iota(shape, dim):
+    return lax.broadcasted_iota(jnp.int32, shape, dim)
+
+
+def fused_kernel(
+    lon_count,
+    state_ref,
+    cot_ref,
+    land_ref,
+    regime_ref,
+    gain1_ref,
+    gain2_ref,
+    proj_ref,
+    outw_ref,
+    bias_ref,
+    up_ref,
+    down_ref,
+    block_ref,
+    gup_ref,
+    gdown_ref,
+    ext,
+    keys,
+    vals,
+    flags,
+    qexp,
+    score,
+    attended,
+    padded,
+    send_c,
+    send_x,
+    got_c,
+    got_x,
+    send_o,
+    got_o,
+    active,
+    pre_act,
+    halo_send,
+    halo_recv,
+    c_send,
+    c_recv,
+    x_send,
+    x_recv,
+    o_send,
+    o_recv,
+    lat_send,
+    lat_recv,
+    fwd_send,
+    fwd_recv,
+):
+    cells, feats = state_ref.shape
+    rows = land_ref.shape[0]
+    heads = bias_ref.shape[0]
+    head_dim = feats // heads
+    local = EXPERTS // lon_count
+    slots = local * 16
+    units = up_ref.shape[1] // local
+    reach = WINDOW // 2
+    f32, bf16 = jnp.float32, jnp.bfloat16
+    lat, lon = lax.axis_index("lat"), lax.axis_index("lon")
+    core_mate = lat + 1 - 2 * lax.rem(lat, 2)
+    x_mate = lax.rem(lat + 2, 4)
+
+    def shifted(dlat, dlon):
+        return (lax.rem(lat + dlat + 4, 4), lax.rem(lon + dlon + lon_count, lon_count))
+
+    near = [(a, b) for a in (-1, 0, 1) for b in (-1, 0, 1) if (a, b) != (0, 0)]
+    barrier = pltpu.get_barrier_semaphore()
+    met = [shifted(*step) for step in near if step[0] != 0]
+    met += [shifted(0, step) for step in range(1, lon_count)] + [(x_mate, lon)]
+    for device in met:
+        pl.semaphore_signal(barrier, inc=1, device_id=device, device_id_type=MESH)
+
+    def remote(source, target, sent, received, device):
+        return pltpu.make_async_remote_copy(
+            src_ref=source,
+            dst_ref=target,
+            send_sem=sent,
+            recv_sem=received,
+            device_id=device,
+            device_id_type=MESH,
+        )
+
+    spread_rows = (iota((cells, rows), 0) // 8 == iota((cells, rows), 1)).astype(bf16)
+    own_col = lax.rem(iota((cells, 8), 0), 8) == iota((cells, 8), 1)
+
+    def column(grid_ref):
+        wide = dot(spread_rows, grid_ref[...].astype(f32).astype(bf16))
+        return jnp.sum(jnp.where(own_col, wide, 0.0), axis=1, keepdims=True)
+
+    land_col = column(land_ref)
+    label_col = column(regime_ref)
+    row_id, col_id = iota((cells, cells), 0), iota((cells, cells), 1)
+    label_row = jnp.sum(jnp.where(row_id == col_id, label_col, 0.0), axis=0, keepdims=True)
+    same = (label_col == label_row).astype(f32)
+    rank_row = jnp.sum(jnp.where(row_id < col_id, same, 0.0), axis=0, keepdims=True)
+    rank_col = jnp.sum(jnp.where(col_id < row_id, same, 0.0), axis=1, keepdims=True)
+    slot_row = (label_row * 16.0 + rank_row).astype(jnp.int32)
+    slot_col = (label_col * 16.0 + rank_col).astype(jnp.int32)
+    all_slots = EXPERTS * 16
+    to_slots = (iota((all_slots, cells), 0) == slot_row).astype(bf16)
+    to_cells = (iota((cells, all_slots), 1) == slot_col).astype(bf16)
+
+    state = state_ref[...].astype(f32)
+    ext[1, HALO : HALO + cells, :feats] = state_ref[...]
+    ext[1, HALO : HALO + cells, feats:] = jnp.broadcast_to(land_col, (cells, LANES)).astype(bf16)
+    tangent = (cot_ref[...].astype(f32) * land_col).astype(bf16)
+    send_c[...] = dot(to_slots, tangent).astype(bf16).reshape(lon_count, slots, feats)
+    got_c[0, pl.ds(lon, 1)] = send_c[pl.ds(lon, 1)]
+
+    pl.semaphore_wait(barrier, len(met))
+
+    halo_copies = []
+    for index, (dlat, dlon) in enumerate(near):
+        if dlat == 0:
+            src, dst = (HALO, cells), (HALO, cells)
+        elif dlat == 1:
+            src, dst = (cells, HALO), (0, HALO)
+        else:
+            src, dst = (HALO, HALO), (HALO + cells, HALO)
+        copy = remote(
+            ext.at[1, pl.ds(*src)],
+            ext.at[1 - dlon, pl.ds(*dst)],
+            halo_send.at[index],
+            halo_recv.at[index],
+            shifted(dlat, dlon),
+        )
+        copy.start()
+        halo_copies.append(copy)
+
+    def to_peers(source, target, sent, received):
+        copies = []
+        for step in range(1, lon_count):
+            device = shifted(0, step)
+            copy = remote(
+                source.at[device[1]], target.at[lon], sent.at[step], received.at[step], device
+            )
+            copy.start()
+            copies.append(copy)
+        return copies
+
+    c_copies = to_peers(send_c, got_c.at[0], c_send, c_recv)
+
+    normed = norm_rows(state, gain1_ref[...])
+    queries = dot(normed, proj_ref[:, :feats]).astype(bf16).astype(f32)
+    head_mask = (iota((heads, feats), 1) // head_dim == iota((heads, feats), 0)).astype(f32)
+    qexp[...] = (
+        (queries[:, None, :] * head_mask[None, :, :]).reshape(cells * heads, feats).astype(bf16)
+    )
+
+    padded[...] = jnp.zeros_like(padded)
+    padded[:, : WINDOW * WINDOW] = bias_ref[...]
+    taps = padded[...]
+    lane = iota((heads, LANES), 1)
+    group, place = lane // 16, lax.rem(lane, 16)
+    base = jnp.zeros((heads, LANES), f32)
+    for a in range(WINDOW):
+        moved = pltpu.roll(taps, 16 * (a + 1) - WINDOW * a, axis=1)
+        base = jnp.where(jnp.logical_and(group == a + 1, place < WINDOW), moved, base)
+    bias_rows, shape_rows, centre_rows = [], [], []
+    key_col = jnp.where(place < 8 + reach, place, place - 16)
+    for q in range(8):
+        rolled = pltpu.roll(base, (q - reach) % LANES, axis=1)
+        if q < reach:
+            wrapped = pltpu.roll(base, q - reach + 16, axis=1)
+            rolled = jnp.where(place >= 8 + reach, wrapped, rolled)
+        bias_rows.append(rolled)
+        inside = jnp.logical_and(jnp.abs(key_col - q) <= reach, group >= 1)
+        shape_rows.append(inside.astype(f32))
+        centre_rows.append(jnp.logical_and(group == reach + 1, place == q).astype(f32))
+    bias = jnp.concatenate(bias_rows, axis=0)
+    inside = jnp.concatenate(shape_rows, axis=0)
+    centre = jnp.concatenate(centre_rows, axis=0)
+    head_rows = jnp.concatenate([head_mask] * 8, axis=0)
+
+    for copy in halo_copies:
+        copy.wait()
+
+    ext_rows = cells + 2 * HALO
+    from_right = lax.rem(iota((ext_rows, 1), 0), 8) < reach
+    around = jnp.where(from_right, ext[2].astype(f32), ext[0].astype(f32))
+    middle = ext[1].astype(f32)
+
+    def interleave(own, other):
+        groups = ext_rows // 8
+        width = own.shape[1]
+        both = jnp.concatenate(
+            [own.reshape(groups, 8, width), other.reshape(groups, 8, width)], axis=1
+        )
+        return both.reshape(2 * ext_rows, width)
+
+    normed_mid = norm_rows(middle[:, :feats], gain1_ref[...])
+    normed_around = norm_rows(around[:, :feats], gain1_ref[...])
+    for target, start in ((keys, feats), (vals, 2 * feats)):
+        weight = proj_ref[:, start : start + feats]
+        target[...] = interleave(dot(normed_mid, weight), dot(normed_around, weight)).astype(bf16)
+    ext_lat = iota((2 * ext_rows, 1), 0) // 16
+    low = jnp.where(lat == 0, HALO // 8, 0)
+    high = jnp.where(lat == 3, (HALO + cells) // 8, ext_rows // 8)
+    on_grid = jnp.logical_and(ext_lat >= low, ext_lat < high)
+    flags[...] = jnp.where(on_grid, interleave(middle[:, feats:], around[:, feats:]), 0.0).astype(
+        bf16
+    )
+
+    per_row = 8 * heads
+    scale = 1.0 / math.sqrt(head_dim)
+    ones = jnp.ones((per_row, LANES), bf16)
+
+    def score_row(i, carry):
+        window = pl.ds(pl.multiple_of(i * 16, 16), LANES)
+        rows_of = pl.ds(pl.multiple_of(i * per_row, per_row), per_row)
+        ocean = dot(ones, flags[window, :], ((1,), (1,)))
+        raw = dot(qexp[rows_of, :], keys[window, :], ((1,), (1,))) * scale + bias
+        valid = jnp.where(ocean > 0.5, inside, centre) > 0.5
+        score[rows_of, :] = jnp.where(valid, raw, -jnp.inf)
+        return carry
+
+    lax.fori_loop(0, rows, score_row, 0, unroll=4)
+    raw = score[...]
+    top = jnp.max(raw, axis=1, keepdims=True)
+    powers = jnp.exp(raw - top)
+    score[...] = powers / jnp.sum(powers, axis=1, keepdims=True)
+
+    def value_row(i, carry):
+        window = pl.ds(pl.multiple_of(i * 16, 16), LANES)
+        rows_of = pl.ds(pl.multiple_of(i * per_row, per_row), per_row)
+        mixed = dot(score[rows_of, :].astype(bf16), vals[window, :]) * head_rows
+        mixed = jnp.sum(mixed.reshape(8, heads, feats), axis=1)
+        attended[pl.ds(pl.multiple_of(i * 8, 8), 8), :] = mixed
+        return carry
+
+    lax.fori_loop(0, rows, value_row, 0, unroll=4)
+
+    residual = (state + dot(attended[...].astype(bf16), outw_ref[...])).astype(bf16).astype(f32)
+    second = norm_rows(residual, gain2_ref[...])
+    send_x[...] = dot(to_slots, second).astype(bf16).reshape(lon_count, slots, feats)
+    x_copies = to_peers(send_x, got_x.at[0], x_send, x_recv)
+    got_x[0, pl.ds(lon, 1)] = send_x[pl.ds(lon, 1)]
+
+    for copy in c_copies:
+        copy.wait()
+    c_core = remote(got_c.at[0], got_c.at[1], lat_send.at[0], lat_recv.at[0], (core_mate, lon))
+    c_far = remote(got_c.at[0], got_c.at[2], lat_send.at[1], lat_recv.at[1], (x_mate, lon))
+    c_far.start()
+    c_core.start()
+    far = []
+    for step in range(lon_count):
+        if step > 0:
+            x_copies[step - 1].wait()
+        source = shifted(0, -step)[1]
+        copy = remote(
+            got_x.at[0, source],
+            got_x.at[2, source],
+            fwd_send.at[step],
+            fwd_recv.at[step],
+            (x_mate, lon),
+        )
+        copy.start()
+        far.append(copy)
+    x_core = remote(got_x.at[0], got_x.at[1], lat_send.at[2], lat_recv.at[2], (core_mate, lon))
+    x_core.start()
+
+    count = lon_count * 16
+
+    def experts_on(band):
+        made = []
+        for e in range(local):
+            x_rows = got_x[band, :, e * 16 : (e + 1) * 16, :].reshape(count, feats)
+            c_rows = got_c[band, :, e * 16 : (e + 1) * 16, :].reshape(count, feats)
+            part = slice(e * units, (e + 1) * units)
+            hidden = dot(x_rows, up_ref[:, part])
+            back = dot(c_rows, down_ref[part, :], ((1,), (1,)))
+            half = 0.5 * (1.0 + lax.erf(hidden * 0.7071067811865476))
+            slope = half + hidden * jnp.exp(-0.5 * hidden * hidden) * 0.3989422804014327
+            act = (hidden * half).astype(bf16)
+            active[e, band * count : (band + 1) * count, :] = act
+            pre_act[e, band * count : (band + 1) * count, :] = (back * slope).astype(bf16)
+            if band == 0:
+                made.append(dot(act, down_ref[part, :]).astype(bf16))
+        return made
+
+    for e, made in enumerate(experts_on(0)):
+        send_o[:, e * 16 : (e + 1) * 16, :] = made.reshape(lon_count, 16, feats)
+    o_copies = to_peers(send_o, got_o, o_send, o_recv)
+    got_o[pl.ds(lon, 1)] = send_o[pl.ds(lon, 1)]
+
+    c_far.wait()
+    c_diag = remote(got_c.at[2], got_c.at[3], lat_send.at[3], lat_recv.at[3], (core_mate, lon))
+    c_diag.start()
+    c_core.wait()
+    x_core.wait()
+    experts_on(1)
+    for copy in far:
+        copy.wait()
+    x_diag = remote(got_x.at[2], got_x.at[3], lat_send.at[4], lat_recv.at[4], (core_mate, lon))
+    x_diag.start()
+    experts_on(2)
+    c_diag.wait()
+    x_diag.wait()
+    experts_on(3)
+
+    for copy in o_copies:
+        copy.wait()
+    returned = got_o[...].reshape(all_slots, feats)
+    block_ref[...] = (land_col * (residual + dot(to_cells, returned))).astype(bf16)
+
+    for e in range(local):
+        x_rows = got_x[:, :, e * 16 : (e + 1) * 16, :].reshape(4 * count, feats)
+        c_rows = got_c[:, :, e * 16 : (e + 1) * 16, :].reshape(4 * count, feats)
+        part = slice(e * units, (e + 1) * units)
+        gup_ref[:, part] = dot(x_rows, pre_act[e], ((0,), (0,)))
+        gdown_ref[part, :] = dot(active[e], c_rows, ((0,), (0,)))
+
+
+def on_device_fused(
+    state,
+    cotangent,
+    land_sea,
+    regime,
+    first_gain,
+    second_gain,
+    project_weight,
+    out_weight,
+    pos_bias,
+    up_weight,
+    down_weight,
+):
+    lat_rows, lon_cols, feats = state.shape
+    cells = lat_rows * lon_cols
+    heads = pos_bias.shape[0]
+    lon_count = lax.axis_size("lon")
+    local = EXPERTS // lon_count
+    slots = local * 16
+    units = up_weight.shape[1] // local
+    ext_rows = cells + 2 * HALO
+    bf16, f32 = jnp.bfloat16, jnp.float32
+    dma = pltpu.SemaphoreType.DMA
+    whole = pl.BlockSpec(memory_space=pltpu.VMEM)
+    block, grad_up, grad_down = pl.pallas_call(
+        functools.partial(fused_kernel, lon_count),
+        out_shape=(
+            jax.ShapeDtypeStruct((cells, feats), bf16),
+            jax.ShapeDtypeStruct(up_weight.shape, f32),
+            jax.ShapeDtypeStruct(down_weight.shape, f32),
+        ),
+        in_specs=[whole] * 11,
+        out_specs=(whole,) * 3,
+        scratch_shapes=[
+            pltpu.VMEM((3, ext_rows, feats + LANES), bf16),
+            pltpu.VMEM((2 * ext_rows, feats), bf16),
+            pltpu.VMEM((2 * ext_rows, feats), bf16),
+            pltpu.VMEM((2 * ext_rows, LANES), bf16),
+            pltpu.VMEM((cells * heads, feats), bf16),
+            pltpu.VMEM((cells * heads, LANES), f32),
+            pltpu.VMEM((cells, feats), f32),
+            pltpu.VMEM((heads, LANES), f32),
+            pltpu.VMEM((lon_count, slots, feats), bf16),
+            pltpu.VMEM((lon_count, slots, feats), bf16),
+            pltpu.VMEM((4, lon_count, slots, feats), bf16),
+            pltpu.VMEM((4, lon_count, slots, feats), bf16),
+            pltpu.VMEM((lon_count, slots, feats), bf16),
+            pltpu.VMEM((lon_count, slots, feats), bf16),
+            pltpu.VMEM((local, 4 * lon_count * 16, units), bf16),
+            pltpu.VMEM((local, 4 * lon_count * 16, units), bf16),
+            dma((8,)),
+            dma((8,)),
+            dma((lon_count,)),
+            dma((lon_count,)),
+            dma((lon_count,)),
+            dma((lon_count,)),
+            dma((lon_count,)),
+            dma((lon_count,)),
+            dma((5,)),
+            dma((5,)),
+            dma((lon_count,)),
+            dma((lon_count,)),
+        ],
+        compiler_params=pltpu.CompilerParams(
+            collective_id=0, has_side_effects=True, vmem_limit_bytes=48 * 1024 * 1024
+        ),
+    )(
+        state.reshape(cells, feats),
+        cotangent.reshape(cells, feats),
+        land_sea,
+        regime.reshape(lat_rows, lon_cols),
+        first_gain.reshape(1, feats),
+        second_gain.reshape(1, feats),
+        project_weight,
+        out_weight,
+        pos_bias,
+        up_weight,
+        down_weight,
+    )
+    return (block.reshape(lat_rows, lon_cols, feats), grad_up, grad_down)
+
+
 def solution(mesh):
     placed = (
         P("lat", "lon", None),
@@ -245,8 +659,10 @@
         P(None, "lon"),
         P("lon", None),
     )
+    lat_count, lon_count = mesh.shape["lat"], mesh.shape["lon"]
+    whole_experts = lat_count == 4 and 4 <= lon_count <= EXPERTS
     return jax.shard_map(
-        on_device,
+        on_device_fused if whole_experts else on_device_general,
         mesh=mesh,
         in_specs=placed,
         out_specs=(P("lat", "lon", None), P(None, "lon"), P("lon", None)),

time: 359 us -> 46.9 us (0.13); the launches traced: 353 us -> 46.4 us
  local copies, waits for them, and re-layouts: 205 us -> 13.9 us
  waiting for transfers between devices: 55.7 us -> 0 us
  other arithmetic: 36.4 us -> 0 us
  starting transfers between devices: 33.3 us -> 0 us
  Pallas kernels: 0 us -> 31.9 us
  between operations: 15.4 us -> 0.65 us
  matrix products: 8.19 us -> 0 us
    reshape x50 -> x1, local copies, waits for them, and re-layouts: 66.5 us -> 0.76 us  [on_device_fused(): regime.reshape(lat_rows, lon_cols)]
    dot_general x49 -> x0, local copies, waits for them, and re-layouts: 61.8 us -> none  [on_device(): jnp.einsum('hxc,hxc->hc', query_heads, key_tap, preferred_element_type=jn...]
    psum x1 -> x0, waiting for transfers between devices: 38.1 us -> none  [on_device(): lax.psum(grad_u.astype(jnp.bfloat16), 'lat').astype(jnp.float32)]
    convert_element_type x55 -> x0, local copies, waits for them, and re-layouts: 36.1 us -> none  [the longest x49 33.7 us: on_device(): value_tap.astype(jnp.float32)]
    pallas_call x0 -> x1, Pallas kernels: none -> 31.9 us  [on_device_fused(): pl.pallas_call(functools.partial(fused_kernel, lon_count), out_shape=(jax...]
    ppermute x8 -> x0, starting transfers between devices: 20.2 us -> none  [the longest x4 13.4 us: extended(): lax.ppermute(head, axis, [((i + 1) % count, i) for i in range(ends)])]
    all_to_all x3 -> x0, waiting for transfers between devices: 17 us -> none  [the longest x1 7.09 us: on_device(): lax.all_to_all(outputs.astype(jnp.bfloat16).reshape(lon_count, per_peer,...]
    unnamed x3 -> x0, other arithmetic: 15 us -> none
  transfers between devices with their start and end apart: 12 -> 0, of which waited for: 5 -> 0; matrix products, arithmetic and copies ran while one was open for 7% -> 0% of each run, Pallas kernels for 0% -> 0%
where the time goes in v1:
time: 46.9 us; the launch traced here: 46.4 us
  Pallas kernels  31.9 us (68%)
  local copies, waits for them, and re-layouts  13.9 us (30%)
  between operations  0.65 us (1%)
    pallas_call x1, Pallas kernels, on_device_fused(): pl.pallas_call(functools.partial(fused_kernel, lon_count), out_shape=(jax...  31.9 us
    unnamed x24, local copies, waits for them, and re-layouts  13.1 us

profile of v1, /device:TPU:0, one launch (start us, length us, event | category | flops | bytes accessed | tf_op | source)
XLA Modules:
  0.0 46.4 jit_solution(10645299831304493478)
XLA Ops:
  0.6 0.8 %copy.14.land_ref = s32[16,8]{1,0:T(8,128)S(1)} copy(s32[16,8]{0,1:T(8,128)} %param.13) | data formatting | bytes 1024 | tf_op args[2]
  1.4 0.8 %copy.15.regime_ref = s32[16,8]{1,0:T(8,128)S(1)} copy(s32[16,8]{0,1:T(8,128)} %bitcast.11) | data formatting | bytes 1024 | tf_op jit(solution)/shard_map/reshape | solution.py:636
  2.1 0.0 copy-start
  2.1 1.2 %copy-done = bf16[256,2048]{1,0:T(8,128)(2,1)S(1)} copy-done((bf16[256,2048]{1,0:T(8,128)(2,1)S(1)}, bf16[256,2048]{1,0:T(8,128)(2,1)}, u32[]{:S(2)}) %copy-start) | copy-done | bytes 1048600
  3.4 0.0 copy-start.1
  3.4 1.2 %copy-done.1 = bf16[2048,256]{1,0:T(8,128)(2,1)S(1)} copy-done((bf16[2048,256]{1,0:T(8,128)(2,1)S(1)}, bf16[2048,256]{1,0:T(8,128)(2,1)}, u32[]{:S(2)}) %copy-start.1) | copy-done | bytes 1048600
  4.6 0.0 copy-start.2
  4.6 1.0 %copy-done.2 = bf16[256,768]{1,0:T(8,128)(2,1)S(1)} copy-done((bf16[256,768]{1,0:T(8,128)(2,1)S(1)}, bf16[256,768]{1,0:T(8,128)(2,1)}, u32[]{:S(2)}) %copy-start.2) | copy-done | bytes 393240
  5.6 0.0 copy-start.3
  5.6 0.9 %copy-done.3 = bf16[256,256]{1,0:T(8,128)(2,1)S(1)} copy-done((bf16[256,256]{1,0:T(8,128)(2,1)S(1)}, bf16[256,256]{1,0:T(8,128)(2,1)}, u32[]{:S(2)}) %copy-start.3) | copy-done | bytes 131096
  6.5 0.0 copy-start.4
  6.5 0.8 %copy-done.4 = bf16[16,8,256]{2,1,0:T(8,128)(2,1)S(1)} copy-done((bf16[16,8,256]{2,1,0:T(8,128)(2,1)S(1)}, bf16[16,8,256]{2,1,0:T(8,128)(2,1)}, u32[]{:S(2)}) %copy-start.4) | copy-done | bytes 65560
  7.3 0.0 copy-start.5
  7.3 0.8 %copy-done.5 = bf16[16,8,256]{2,1,0:T(8,128)(2,1)S(1)} copy-done((bf16[16,8,256]{2,1,0:T(8,128)(2,1)S(1)}, bf16[16,8,256]{2,1,0:T(8,128)(2,1)}, u32[]{:S(2)}) %copy-start.5) | copy-done | bytes 65560
  8.2 0.0 copy-start.6
  8.2 0.7 %copy-done.6 = f32[8,49]{1,0:T(8,128)S(1)} copy-done((f32[8,49]{1,0:T(8,128)S(1)}, f32[8,49]{1,0:T(8,128)}, u32[]{:S(2)}) %copy-start.6) | copy-done | bytes 1592
  8.9 0.0 copy-start.7
  8.9 0.7 %copy-done.7 = f32[256]{0:T(256)S(1)} copy-done((f32[256]{0:T(256)S(1)}, f32[256]{0:T(256)}, u32[]{:S(2)}) %copy-start.7) | copy-done | bytes 1048
  9.5 0.0 copy-start.8
  9.5 0.7 %copy-done.8 = f32[256]{0:T(256)S(1)} copy-done((f32[256]{0:T(256)S(1)}, f32[256]{0:T(256)}, u32[]{:S(2)}) %copy-start.8) | copy-done | bytes 1048
  10.2 31.9 %shard_map.130 = (bf16[128,256]{1,0:T(8,128)(2,1)S(1)}, f32[256,2048]{1,0:T(8,128)S(1)}, f32[2048,256]{1,0:T(8,128)}) custom-call(bf16[128,256]{1,0:T(8,128)(2,1)S(1)} %bitcast.6, bf16[128,256]{1,0:T(8,128)(2,1)S(1)} %bitcast.7, s32[16,8]{1,0:T(8,128)S(1)} %copy.14.land_ref, s32[16,8]{1,0:T(8,128)S(1)} %copy.15.regime_ref, f32[1,256]{1,0:T(1,128)S(1)} %bitcast.9, ...), custom_call_target="tpu_custom_call" | custom-call | tf_op jit(solution)/shard_map/pallas_call | solution.py:590
  42.1 0.6 %copy.19 = bf16[16,8,256]{2,1,0:T(8,128)(2,1)} copy(bf16[16,8,256]{2,1,0:T(8,128)(2,1)S(1)} %bitcast.8) | data formatting | bytes 131072
  42.7 0.0 copy-start.9
  42.8 1.3 %copy.20 = f32[256,2048]{1,0:T(8,128)} copy(f32[256,2048]{1,0:T(8,128)S(1)} %get-tuple-element.13) | data formatting | bytes 4194304
  44.1 1.0 %copy-done.9 = f32[2048,256]{1,0:T(8,128)S(1)} copy-done((f32[2048,256]{1,0:T(8,128)S(1)}, f32[2048,256]{1,0:T(8,128)}, u32[]{:S(2)}) %copy-start.9) | copy-done | bytes 2097176
  45.1 1.3 %copy.21 = f32[2048,256]{1,0:T(8,128)} copy(f32[2048,256]{1,0:T(8,128)S(1)} %copy-done.9) | data formatting | bytes 4194304
Async XLA Ops:
  2.1 1.2 %copy-start = (bf16[256,2048]{1,0:T(8,128)(2,1)S(1)}, bf16[256,2048]{1,0:T(8,128)(2,1)}, u32[]{:S(2)}) copy-start(bf16[256,2048]{1,0:T(8,128)(2,1)} %up_ref.1) | copy-start | bytes 3145732
  3.4 1.2 %copy-start.1 = (bf16[2048,256]{1,0:T(8,128)(2,1)S(1)}, bf16[2048,256]{1,0:T(8,128)(2,1)}, u32[]{:S(2)}) copy-start(bf16[2048,256]{1,0:T(8,128)(2,1)} %down_ref.1) | copy-start | bytes 3145732
  4.6 1.0 %copy-start.2 = (bf16[256,768]{1,0:T(8,128)(2,1)S(1)}, bf16[256,768]{1,0:T(8,128)(2,1)}, u32[]{:S(2)}) copy-start(bf16[256,768]{1,0:T(8,128)(2,1)} %proj_ref.1) | copy-start | bytes 1179652
  5.6 0.9 %copy-start.3 = (bf16[256,256]{1,0:T(8,128)(2,1)S(1)}, bf16[256,256]{1,0:T(8,128)(2,1)}, u32[]{:S(2)}) copy-start(bf16[256,256]{1,0:T(8,128)(2,1)} %outw_ref.1) | copy-start | bytes 393220
  6.5 0.8 %copy-start.4 = (bf16[16,8,256]{2,1,0:T(8,128)(2,1)S(1)}, bf16[16,8,256]{2,1,0:T(8,128)(2,1)}, u32[]{:S(2)}) copy-start(bf16[16,8,256]{2,1,0:T(8,128)(2,1)} %param.11) | copy-start | bytes 196612
  7.3 0.8 %copy-start.5 = (bf16[16,8,256]{2,1,0:T(8,128)(2,1)S(1)}, bf16[16,8,256]{2,1,0:T(8,128)(2,1)}, u32[]{:S(2)}) copy-start(bf16[16,8,256]{2,1,0:T(8,128)(2,1)} %param.12) | copy-start | bytes 196612
  8.2 0.7 %copy-start.6 = (f32[8,49]{1,0:T(8,128)S(1)}, f32[8,49]{1,0:T(8,128)}, u32[]{:S(2)}) copy-start(f32[8,49]{1,0:T(8,128)} %bias_ref.1) | copy-start | bytes 4708
  8.9 0.7 %copy-start.7 = (f32[256]{0:T(256)S(1)}, f32[256]{0:T(256)}, u32[]{:S(2)}) copy-start(f32[256]{0:T(256)} %param.15) | copy-start | bytes 3076
  9.5 0.7 %copy-start.8 = (f32[256]{0:T(256)S(1)}, f32[256]{0:T(256)}, u32[]{:S(2)}) copy-start(f32[256]{0:T(256)} %param.16) | copy-start | bytes 3076
  42.7 2.3 %copy-start.9 = (f32[2048,256]{1,0:T(8,128)S(1)}, f32[2048,256]{1,0:T(8,128)}, u32[]{:S(2)}) copy-start(f32[2048,256]{1,0:T(8,128)} %get-tuple-element.14) | copy-start | bytes 6291460

commit v2 on v1

--- a/solution.py
+++ b/solution.py
@@ -256,6 +256,24 @@
 
 def fused_kernel(
     lon_count,
+    state_hbm,
+    cot_hbm,
+    land_hbm,
+    regime_hbm,
+    gain1_hbm,
+    gain2_hbm,
+    proj_hbm,
+    outw_hbm,
+    bias_hbm,
+    up_hbm,
+    down_hbm,
+    x_hbm,
+    c_hbm,
+    active_hbm,
+    pre_hbm,
+    kept_hbm,
+    pick_hbm,
+    returned_hbm,
     state_ref,
     cot_ref,
     land_ref,
@@ -267,9 +285,14 @@
     bias_ref,
     up_ref,
     down_ref,
-    block_ref,
-    gup_ref,
-    gdown_ref,
+    load_sem,
+    x_out,
+    c_out,
+    active,
+    pre_act,
+    kept_out,
+    pick_out,
+    store_sem,
     ext,
     keys,
     vals,
@@ -284,8 +307,6 @@
     got_x,
     send_o,
     got_o,
-    active,
-    pre_act,
     halo_send,
     halo_recv,
     c_send,
@@ -300,7 +321,7 @@
     fwd_recv,
 ):
     cells, feats = state_ref.shape
-    rows = land_ref.shape[0]
+    rows = land_ref.shape[1]
     heads = bias_ref.shape[0]
     head_dim = feats // heads
     local = EXPERTS // lon_count
@@ -322,6 +343,27 @@
     for device in met:
         pl.semaphore_signal(barrier, inc=1, device_id=device, device_id_type=MESH)
 
+    loads = {}
+    for index, (source, target) in enumerate(
+        (
+            (land_hbm, land_ref),
+            (regime_hbm, regime_ref),
+            (state_hbm, state_ref),
+            (cot_hbm, cot_ref),
+            (gain1_hbm, gain1_ref),
+            (proj_hbm, proj_ref),
+            (bias_hbm, bias_ref),
+            (gain2_hbm, gain2_ref),
+            (outw_hbm, outw_ref),
+            (up_hbm, up_ref),
+            (down_hbm, down_ref),
+        )
+    ):
+        loads[index] = pltpu.make_async_copy(source, target, load_sem.at[index])
+        loads[index].start()
+    loads[0].wait()
+    loads[1].wait()
+
     def remote(source, target, sent, received, device):
         return pltpu.make_async_remote_copy(
             src_ref=source,
@@ -336,7 +378,7 @@
     own_col = lax.rem(iota((cells, 8), 0), 8) == iota((cells, 8), 1)
 
     def column(grid_ref):
-        wide = dot(spread_rows, grid_ref[...].astype(f32).astype(bf16))
+        wide = dot(spread_rows, grid_ref[...].astype(f32).astype(bf16), ((1,), (1,)))
         return jnp.sum(jnp.where(own_col, wide, 0.0), axis=1, keepdims=True)
 
     land_col = column(land_ref)
@@ -352,6 +394,8 @@
     to_slots = (iota((all_slots, cells), 0) == slot_row).astype(bf16)
     to_cells = (iota((cells, all_slots), 1) == slot_col).astype(bf16)
 
+    loads[2].wait()
+    loads[3].wait()
     state = state_ref[...].astype(f32)
     ext[1, HALO : HALO + cells, :feats] = state_ref[...]
     ext[1, HALO : HALO + cells, feats:] = jnp.broadcast_to(land_col, (cells, LANES)).astype(bf16)
@@ -391,6 +435,9 @@
         return copies
 
     c_copies = to_peers(send_c, got_c.at[0], c_send, c_recv)
+
+    for index in (4, 5, 6):
+        loads[index].wait()
 
     normed = norm_rows(state, gain1_ref[...])
     queries = dot(normed, proj_ref[:, :feats]).astype(bf16).astype(f32)
@@ -455,12 +502,12 @@
 
     per_row = 8 * heads
     scale = 1.0 / math.sqrt(head_dim)
-    ones = jnp.ones((per_row, LANES), bf16)
+    ones = jnp.ones((8, LANES), bf16)
 
     def score_row(i, carry):
         window = pl.ds(pl.multiple_of(i * 16, 16), LANES)
         rows_of = pl.ds(pl.multiple_of(i * per_row, per_row), per_row)
-        ocean = dot(ones, flags[window, :], ((1,), (1,)))
+        ocean = dot(ones, flags[window, :], ((1,), (1,)))[:1]
         raw = dot(qexp[rows_of, :], keys[window, :], ((1,), (1,))) * scale + bias
         valid = jnp.where(ocean > 0.5, inside, centre) > 0.5
         score[rows_of, :] = jnp.where(valid, raw, -jnp.inf)
@@ -482,6 +529,8 @@
 
     lax.fori_loop(0, rows, value_row, 0, unroll=4)
 
+    loads[7].wait()
+    loads[8].wait()
     residual = (state + dot(attended[...].astype(bf16), outw_ref[...])).astype(bf16).astype(f32)
     second = norm_rows(residual, gain2_ref[...])
     send_x[...] = dot(to_slots, second).astype(bf16).reshape(lon_count, slots, feats)
@@ -511,21 +560,45 @@
     x_core = remote(got_x.at[0], got_x.at[1], lat_send.at[2], lat_recv.at[2], (core_mate, lon))
     x_core.start()
 
+    loads[9].wait()
+    loads[10].wait()
     count = lon_count * 16
+
+    stores = []
+
+    def store(source, target):
+        copy = pltpu.make_async_copy(source, target, store_sem.at[len(stores)])
+        copy.start()
+        stores.append(copy)
+
+    kept_out[...] = (land_col * residual).astype(bf16)
+    pick_out[...] = (land_col * to_cells.astype(f32)).astype(bf16)
+    store(kept_out, kept_hbm)
+    store(pick_out, pick_hbm)
 
     def experts_on(band):
         made = []
         for e in range(local):
             x_rows = got_x[band, :, e * 16 : (e + 1) * 16, :].reshape(count, feats)
             c_rows = got_c[band, :, e * 16 : (e + 1) * 16, :].reshape(count, feats)
+            here = slice(band * count, (band + 1) * count)
+            x_out[e, here, :] = x_rows
+            c_out[e, here, :] = c_rows
             part = slice(e * units, (e + 1) * units)
             hidden = dot(x_rows, up_ref[:, part])
             back = dot(c_rows, down_ref[part, :], ((1,), (1,)))
             half = 0.5 * (1.0 + lax.erf(hidden * 0.7071067811865476))
             slope = half + hidden * jnp.exp(-0.5 * hidden * hidden) * 0.3989422804014327
             act = (hidden * half).astype(bf16)
-            active[e, band * count : (band + 1) * count, :] = act
-            pre_act[e, band * count : (band + 1) * count, :] = (back * slope).astype(bf16)
+            active[e, here, :] = act
+            pre_act[e, here, :] = (back * slope).astype(bf16)
+            for made_here, target in (
+                (x_out, x_hbm),
+                (c_out, c_hbm),
+                (active, active_hbm),
+                (pre_act, pre_hbm),
+            ):
+                store(made_here.at[e, here], target.at[e, here])
             if band == 0:
                 made.append(dot(act, down_ref[part, :]).astype(bf16))
         return made
@@ -552,15 +625,19 @@
 
     for copy in o_copies:
         copy.wait()
-    returned = got_o[...].reshape(all_slots, feats)
-    block_ref[...] = (land_col * (residual + dot(to_cells, returned))).astype(bf16)
-
-    for e in range(local):
-        x_rows = got_x[:, :, e * 16 : (e + 1) * 16, :].reshape(4 * count, feats)
-        c_rows = got_c[:, :, e * 16 : (e + 1) * 16, :].reshape(4 * count, feats)
-        part = slice(e * units, (e + 1) * units)
-        gup_ref[:, part] = dot(x_rows, pre_act[e], ((0,), (0,)))
-        gdown_ref[part, :] = dot(active[e], c_rows, ((0,), (0,)))
+    store(got_o, returned_hbm)
+    for copy in stores:
+        copy.wait()
+
+
+def gradient_kernel(
+    x_ref, c_ref, active_ref, pre_ref, kept_ref, pick_ref, returned_ref, block_ref, gup_ref, gdown_ref
+):
+    block_ref[...] = (kept_ref[...].astype(jnp.float32) + dot(pick_ref[...], returned_ref[...])).astype(
+        jnp.bfloat16
+    )
+    gup_ref[...] = dot(x_ref[0], pre_ref[0], ((0,), (0,)))
+    gdown_ref[...] = dot(active_ref[0], c_ref[0], ((0,), (0,)))
 
 
 def on_device_fused(
@@ -586,17 +663,44 @@
     ext_rows = cells + 2 * HALO
     bf16, f32 = jnp.bfloat16, jnp.float32
     dma = pltpu.SemaphoreType.DMA
-    whole = pl.BlockSpec(memory_space=pltpu.VMEM)
-    block, grad_up, grad_down = pl.pallas_call(
+    hbm = pl.BlockSpec(memory_space=pltpu.HBM)
+    all_rows = 4 * lon_count * 16
+    operands = (
+        state.reshape(cells, feats),
+        cotangent.reshape(cells, feats),
+        land_sea.T,
+        regime.reshape(lat_rows, lon_cols).T,
+        first_gain.reshape(1, feats),
+        second_gain.reshape(1, feats),
+        project_weight,
+        out_weight,
+        pos_bias,
+        up_weight,
+        down_weight,
+    )
+    made = pl.pallas_call(
         functools.partial(fused_kernel, lon_count),
         out_shape=(
+            jax.ShapeDtypeStruct((local, all_rows, feats), bf16),
+            jax.ShapeDtypeStruct((local, all_rows, feats), bf16),
+            jax.ShapeDtypeStruct((local, all_rows, units), bf16),
+            jax.ShapeDtypeStruct((local, all_rows, units), bf16),
             jax.ShapeDtypeStruct((cells, feats), bf16),
-            jax.ShapeDtypeStruct(up_weight.shape, f32),
-            jax.ShapeDtypeStruct(down_weight.shape, f32),
+            jax.ShapeDtypeStruct((cells, EXPERTS * 16), bf16),
+            jax.ShapeDtypeStruct((lon_count, slots, feats), bf16),
         ),
-        in_specs=[whole] * 11,
-        out_specs=(whole,) * 3,
+        in_specs=[hbm] * 11,
+        out_specs=(hbm,) * 7,
         scratch_shapes=[
+            *(pltpu.VMEM(operand.shape, operand.dtype) for operand in operands),
+            dma((11,)),
+            pltpu.VMEM((local, all_rows, feats), bf16),
+            pltpu.VMEM((local, all_rows, feats), bf16),
+            pltpu.VMEM((local, all_rows, units), bf16),
+            pltpu.VMEM((local, all_rows, units), bf16),
+            pltpu.VMEM((cells, feats), bf16),
+            pltpu.VMEM((cells, EXPERTS * 16), bf16),
+            dma((3 + 16 * local,)),
             pltpu.VMEM((3, ext_rows, feats + LANES), bf16),
             pltpu.VMEM((2 * ext_rows, feats), bf16),
             pltpu.VMEM((2 * ext_rows, feats), bf16),
@@ -611,8 +715,6 @@
             pltpu.VMEM((4, lon_count, slots, feats), bf16),
             pltpu.VMEM((lon_count, slots, feats), bf16),
             pltpu.VMEM((lon_count, slots, feats), bf16),
-            pltpu.VMEM((local, 4 * lon_count * 16, units), bf16),
-            pltpu.VMEM((local, 4 * lon_count * 16, units), bf16),
             dma((8,)),
             dma((8,)),
             dma((lon_count,)),
@@ -627,21 +729,35 @@
             dma((lon_count,)),
         ],
         compiler_params=pltpu.CompilerParams(
-            collective_id=0, has_side_effects=True, vmem_limit_bytes=48 * 1024 * 1024
+            collective_id=0, has_side_effects=True, vmem_limit_bytes=56 * 1024 * 1024
         ),
-    )(
-        state.reshape(cells, feats),
-        cotangent.reshape(cells, feats),
-        land_sea,
-        regime.reshape(lat_rows, lon_cols),
-        first_gain.reshape(1, feats),
-        second_gain.reshape(1, feats),
-        project_weight,
-        out_weight,
-        pos_bias,
-        up_weight,
-        down_weight,
-    )
+    )(*operands)
+    wide = units // 2
+    halves = units // wide
+    block, grad_up, grad_down = pl.pallas_call(
+        gradient_kernel,
+        grid=(local, halves),
+        out_shape=(
+            jax.ShapeDtypeStruct((cells, feats), bf16),
+            jax.ShapeDtypeStruct(up_weight.shape, f32),
+            jax.ShapeDtypeStruct(down_weight.shape, f32),
+        ),
+        in_specs=[
+            pl.BlockSpec((1, all_rows, feats), lambda e, u: (e, 0, 0)),
+            pl.BlockSpec((1, all_rows, feats), lambda e, u: (e, 0, 0)),
+            pl.BlockSpec((1, all_rows, wide), lambda e, u: (e, 0, u)),
+            pl.BlockSpec((1, all_rows, wide), lambda e, u: (e, 0, u)),
+            pl.BlockSpec((cells, feats), lambda e, u: (0, 0)),
+            pl.BlockSpec((cells, EXPERTS * 16), lambda e, u: (0, 0)),
+            pl.BlockSpec((EXPERTS * 16, feats), lambda e, u: (0, 0)),
+        ],
+        out_specs=(
+            pl.BlockSpec((cells, feats), lambda e, u: (0, 0)),
+            pl.BlockSpec((feats, wide), lambda e, u: (0, e * halves + u)),
+            pl.BlockSpec((wide, feats), lambda e, u: (e * halves + u, 0)),
+        ),
+        compiler_params=pltpu.CompilerParams(vmem_limit_bytes=56 * 1024 * 1024),
+    )(*made[:6], made[6].reshape(EXPERTS * 16, feats))
     return (block.reshape(lat_rows, lon_cols, feats), grad_up, grad_down)
 
 

time: 46.9 us -> 36.9 us (0.79)
  local copies, waits for them, and re-layouts: 13.9 us -> 0 us
  Pallas kernels: 31.9 us -> 36 us
    unnamed x24 -> x0, local copies, waits for them, and re-layouts: 13.1 us -> none
    pallas_call x0 -> x1, Pallas kernels: none -> 5.73 us  [on_device_fused(): pl.pallas_call(gradient_kernel, grid=(local, halves), out_shape=(jax.Shap...]
    pallas_call x1, Pallas kernels: 31.9 us -> 30.3 us  [on_device_fused(): pl.pallas_call(functools.partial(fused_kernel, lon_count), out_shape=(jax...]
    reshape x1 -> x0, local copies, waits for them, and re-layouts: 0.76 us -> none  [on_device_fused(): regime.reshape(lat_rows, lon_cols)]
where the time goes in v2:
time: 36.9 us; the launch traced here: 36.7 us
  Pallas kernels  36 us (98%)
  between operations  0.64 us (2%)
    pallas_call x1, Pallas kernels, on_device_fused(): pl.pallas_call(functools.partial(fused_kernel, lon_count), out_shape=(jax...  30.3 us
    pallas_call x1, Pallas kernels, on_device_fused(): pl.pallas_call(gradient_kernel, grid=(local, halves), out_shape=(jax.Shap...  5.73 us

profile of v2, /device:TPU:0, one launch (start us, length us, event | category | flops | bytes accessed | tf_op | source)
XLA Modules:
  0.0 36.7 jit_solution(5600813874517932275)
XLA Ops:
  0.6 30.3 %shard_map.130 = (bf16[2,512,256]{2,1,0:T(8,128)(2,1)}, bf16[2,512,256]{2,1,0:T(8,128)(2,1)}, bf16[2,512,1024]{2,1,0:T(8,128)(2,1)}, bf16[2,512,1024]{2,1,0:T(8,...) custom-call(bf16[128,256]{1,0:T(8,128)(2,1)} %bitcast.11, ...), custom_call_target="tpu_custom_call" | custom-call | tf_op jit(solution)/shard_map/pallas_call | solution.py:681
  30.9 5.7 %shard_map.131 = (bf16[128,256]{1,0:T(8,128)(2,1)}, f32[256,2048]{1,0:T(8,128)}, f32[2048,256]{1,0:T(8,128)}) custom-call(bf16[2,512,256]{2,1,0:T(8,128)(2,1)} %get-tuple-element.13.x_ref, bf16[2,512,256]{2,1,0:T(8,128)(2,1)} %get-tuple-element.14.c_ref, bf16[2,512,1024]{2,1,0:T(8,128)(2,1)} %get-tuple-element.15.active_ref, ...), custom_call_target="tpu_custom_call" | custom-call | tf_op jit(solution)/shard_map/pallas_call | solution.py:737

commit v3 on v2

--- a/solution.py
+++ b/solution.py
@@ -254,6 +254,19 @@
     return lax.broadcasted_iota(jnp.int32, shape, dim)
 
 
+def gelu_parts(hidden):
+    bell = jnp.exp(-0.5 * hidden * hidden)
+    depth = 1.0 + 0.3275911 * 0.7071067811865476 * jnp.abs(hidden)
+    near = pl.reciprocal(depth, approx=True)
+    near = near * (2.0 - depth * near)
+    series = 0.5 * 1.061405429
+    for factor in (-1.453152027, 1.421413741, -0.284496736, 0.254829592):
+        series = series * near + 0.5 * factor
+    tail = series * near * bell
+    half = jnp.where(hidden >= 0.0, 1.0 - tail, tail)
+    return (hidden * half, half + hidden * bell * 0.3989422804014327)
+
+
 def fused_kernel(
     lon_count,
     state_hbm,
@@ -298,7 +311,7 @@
     vals,
     flags,
     qexp,
-    score,
+    own_kv,
     attended,
     padded,
     send_c,
@@ -440,6 +453,7 @@
         loads[index].wait()
 
     normed = norm_rows(state, gain1_ref[...])
+    own_kv[...] = dot(normed, proj_ref[:, feats:])
     queries = dot(normed, proj_ref[:, :feats]).astype(bf16).astype(f32)
     head_mask = (iota((heads, feats), 1) // head_dim == iota((heads, feats), 0)).astype(f32)
     qexp[...] = (
@@ -478,6 +492,7 @@
     from_right = lax.rem(iota((ext_rows, 1), 0), 8) < reach
     around = jnp.where(from_right, ext[2].astype(f32), ext[0].astype(f32))
     middle = ext[1].astype(f32)
+    ends = jnp.concatenate([middle[:HALO], middle[HALO + cells :]], axis=0)
 
     def interleave(own, other):
         groups = ext_rows // 8
@@ -487,11 +502,16 @@
         )
         return both.reshape(2 * ext_rows, width)
 
-    normed_mid = norm_rows(middle[:, :feats], gain1_ref[...])
-    normed_around = norm_rows(around[:, :feats], gain1_ref[...])
-    for target, start in ((keys, feats), (vals, 2 * feats)):
-        weight = proj_ref[:, start : start + feats]
-        target[...] = interleave(dot(normed_mid, weight), dot(normed_around, weight)).astype(bf16)
+    normed_far = jnp.concatenate(
+        [norm_rows(ends[:, :feats], gain1_ref[...]), norm_rows(around[:, :feats], gain1_ref[...])],
+        axis=0,
+    )
+    for target, start in ((keys, 0), (vals, feats)):
+        far_part = dot(normed_far, proj_ref[:, feats + start : 2 * feats + start])
+        own = jnp.concatenate(
+            [far_part[:HALO], own_kv[:, start : start + feats], far_part[HALO : 2 * HALO]], axis=0
+        )
+        target[...] = interleave(own, far_part[2 * HALO :]).astype(bf16)
     ext_lat = iota((2 * ext_rows, 1), 0) // 16
     low = jnp.where(lat == 0, HALO // 8, 0)
     high = jnp.where(lat == 3, (HALO + cells) // 8, ext_rows // 8)
@@ -500,34 +520,39 @@
         bf16
     )
 
+    for copy in c_copies:
+        copy.wait()
+    c_core = remote(got_c.at[0], got_c.at[1], lat_send.at[0], lat_recv.at[0], (core_mate, lon))
+    c_far = remote(got_c.at[0], got_c.at[2], lat_send.at[1], lat_recv.at[1], (x_mate, lon))
+    c_far.start()
+    c_core.start()
+
     per_row = 8 * heads
     scale = 1.0 / math.sqrt(head_dim)
     ones = jnp.ones((8, LANES), bf16)
 
-    def score_row(i, carry):
-        window = pl.ds(pl.multiple_of(i * 16, 16), LANES)
-        rows_of = pl.ds(pl.multiple_of(i * per_row, per_row), per_row)
-        ocean = dot(ones, flags[window, :], ((1,), (1,)))[:1]
-        raw = dot(qexp[rows_of, :], keys[window, :], ((1,), (1,))) * scale + bias
-        valid = jnp.where(ocean > 0.5, inside, centre) > 0.5
-        score[rows_of, :] = jnp.where(valid, raw, -jnp.inf)
+    batch = 4
+
+    def attend(i, carry):
+        windows = [pl.ds(pl.multiple_of((i * batch + k) * 16, 16), LANES) for k in range(batch)]
+        rows_of = pl.ds(pl.multiple_of(i * batch * per_row, batch * per_row), batch * per_row)
+        rows_q = qexp[rows_of, :]
+        parts = []
+        for k, window in enumerate(windows):
+            ocean = dot(ones, flags[window, :], ((1,), (1,)))[:1]
+            raw = dot(rows_q[k * per_row : (k + 1) * per_row], keys[window, :], ((1,), (1,)))
+            valid = jnp.where(ocean > 0.5, inside, centre) > 0.5
+            parts.append(jnp.where(valid, raw * scale + bias, -jnp.inf))
+        raw = jnp.concatenate(parts, axis=0)
+        powers = jnp.exp(raw - jnp.max(raw, axis=1, keepdims=True))
+        weights = (powers / jnp.sum(powers, axis=1, keepdims=True)).astype(bf16)
+        for k, window in enumerate(windows):
+            mixed = dot(weights[k * per_row : (k + 1) * per_row], vals[window, :]) * head_rows
+            mixed = jnp.sum(mixed.reshape(8, heads, feats), axis=1)
+            attended[pl.ds(pl.multiple_of((i * batch + k) * 8, 8), 8), :] = mixed
         return carry
 
-    lax.fori_loop(0, rows, score_row, 0, unroll=4)
-    raw = score[...]
-    top = jnp.max(raw, axis=1, keepdims=True)
-    powers = jnp.exp(raw - top)
-    score[...] = powers / jnp.sum(powers, axis=1, keepdims=True)
-
-    def value_row(i, carry):
-        window = pl.ds(pl.multiple_of(i * 16, 16), LANES)
-        rows_of = pl.ds(pl.multiple_of(i * per_row, per_row), per_row)
-        mixed = dot(score[rows_of, :].astype(bf16), vals[window, :]) * head_rows
-        mixed = jnp.sum(mixed.reshape(8, heads, feats), axis=1)
-        attended[pl.ds(pl.multiple_of(i * 8, 8), 8), :] = mixed
-        return carry
-
-    lax.fori_loop(0, rows, value_row, 0, unroll=4)
+    lax.fori_loop(0, rows // batch, attend, 0)
 
     loads[7].wait()
     loads[8].wait()
@@ -537,12 +562,6 @@
     x_copies = to_peers(send_x, got_x.at[0], x_send, x_recv)
     got_x[0, pl.ds(lon, 1)] = send_x[pl.ds(lon, 1)]
 
-    for copy in c_copies:
-        copy.wait()
-    c_core = remote(got_c.at[0], got_c.at[1], lat_send.at[0], lat_recv.at[0], (core_mate, lon))
-    c_far = remote(got_c.at[0], got_c.at[2], lat_send.at[1], lat_recv.at[1], (x_mate, lon))
-    c_far.start()
-    c_core.start()
     far = []
     for step in range(lon_count):
         if step > 0:
@@ -582,25 +601,25 @@
             x_rows = got_x[band, :, e * 16 : (e + 1) * 16, :].reshape(count, feats)
             c_rows = got_c[band, :, e * 16 : (e + 1) * 16, :].reshape(count, feats)
             here = slice(band * count, (band + 1) * count)
-            x_out[e, here, :] = x_rows
+            x_out[e, :, here] = x_rows.T
             c_out[e, here, :] = c_rows
-            part = slice(e * units, (e + 1) * units)
-            hidden = dot(x_rows, up_ref[:, part])
-            back = dot(c_rows, down_ref[part, :], ((1,), (1,)))
-            half = 0.5 * (1.0 + lax.erf(hidden * 0.7071067811865476))
-            slope = half + hidden * jnp.exp(-0.5 * hidden * hidden) * 0.3989422804014327
-            act = (hidden * half).astype(bf16)
-            active[e, here, :] = act
-            pre_act[e, here, :] = (back * slope).astype(bf16)
-            for made_here, target in (
-                (x_out, x_hbm),
-                (c_out, c_hbm),
-                (active, active_hbm),
-                (pre_act, pre_hbm),
-            ):
-                store(made_here.at[e, here], target.at[e, here])
+            total = jnp.zeros((count, feats), f32)
+            for start in range(e * units, (e + 1) * units, feats):
+                part = slice(start, start + feats)
+                spot = slice(start - e * units, start - e * units + feats)
+                act, slope = gelu_parts(dot(x_rows, up_ref[:, part]))
+                act = act.astype(bf16)
+                back = dot(c_rows, down_ref[part, :], ((1,), (1,)))
+                active[e, spot, here] = act.T
+                pre_act[e, here, spot] = (back * slope).astype(bf16)
+                if band == 0:
+                    total += dot(act, down_ref[part, :])
+            store(x_out.at[e, :, here], x_hbm.at[e, :, here])
+            store(c_out.at[e, here], c_hbm.at[e, here])
+            store(active.at[e, :, here], active_hbm.at[e, :, here])
+            store(pre_act.at[e, here], pre_hbm.at[e, here])
             if band == 0:
-                made.append(dot(act, down_ref[part, :]).astype(bf16))
+                made.append(total.astype(bf16))
         return made
 
     for e, made in enumerate(experts_on(0)):
@@ -636,8 +655,8 @@
     block_ref[...] = (kept_ref[...].astype(jnp.float32) + dot(pick_ref[...], returned_ref[...])).astype(
         jnp.bfloat16
     )
-    gup_ref[...] = dot(x_ref[0], pre_ref[0], ((0,), (0,)))
-    gdown_ref[...] = dot(active_ref[0], c_ref[0], ((0,), (0,)))
+    gup_ref[...] = dot(x_ref[0], pre_ref[0])
+    gdown_ref[...] = dot(active_ref[0], c_ref[0])
 
 
 def on_device_fused(
@@ -681,9 +700,9 @@
     made = pl.pallas_call(
         functools.partial(fused_kernel, lon_count),
         out_shape=(
+            jax.ShapeDtypeStruct((local, feats, all_rows), bf16),
             jax.ShapeDtypeStruct((local, all_rows, feats), bf16),
-            jax.ShapeDtypeStruct((local, all_rows, feats), bf16),
-            jax.ShapeDtypeStruct((local, all_rows, units), bf16),
+            jax.ShapeDtypeStruct((local, units, all_rows), bf16),
             jax.ShapeDtypeStruct((local, all_rows, units), bf16),
             jax.ShapeDtypeStruct((cells, feats), bf16),
             jax.ShapeDtypeStruct((cells, EXPERTS * 16), bf16),
@@ -694,9 +713,9 @@
         scratch_shapes=[
             *(pltpu.VMEM(operand.shape, operand.dtype) for operand in operands),
             dma((11,)),
+            pltpu.VMEM((local, feats, all_rows), bf16),
             pltpu.VMEM((local, all_rows, feats), bf16),
-            pltpu.VMEM((local, all_rows, feats), bf16),
-            pltpu.VMEM((local, all_rows, units), bf16),
+            pltpu.VMEM((local, units, all_rows), bf16),
             pltpu.VMEM((local, all_rows, units), bf16),
             pltpu.VMEM((cells, feats), bf16),
             pltpu.VMEM((cells, EXPERTS * 16), bf16),
@@ -706,7 +725,7 @@
             pltpu.VMEM((2 * ext_rows, feats), bf16),
             pltpu.VMEM((2 * ext_rows, LANES), bf16),
             pltpu.VMEM((cells * heads, feats), bf16),
-            pltpu.VMEM((cells * heads, LANES), f32),
+            pltpu.VMEM((cells, 2 * feats), f32),
             pltpu.VMEM((cells, feats), f32),
             pltpu.VMEM((heads, LANES), f32),
             pltpu.VMEM((lon_count, slots, feats), bf16),
@@ -743,9 +762,9 @@
             jax.ShapeDtypeStruct(down_weight.shape, f32),
         ),
         in_specs=[
+            pl.BlockSpec((1, feats, all_rows), lambda e, u: (e, 0, 0)),
             pl.BlockSpec((1, all_rows, feats), lambda e, u: (e, 0, 0)),
-            pl.BlockSpec((1, all_rows, feats), lambda e, u: (e, 0, 0)),
-            pl.BlockSpec((1, all_rows, wide), lambda e, u: (e, 0, u)),
+            pl.BlockSpec((1, wide, all_rows), lambda e, u: (e, u, 0)),
             pl.BlockSpec((1, all_rows, wide), lambda e, u: (e, 0, u)),
             pl.BlockSpec((cells, feats), lambda e, u: (0, 0)),
             pl.BlockSpec((cells, EXPERTS * 16), lambda e, u: (0, 0)),

time: 36.9 us -> 37.9 us (1.027)
  Pallas kernels: 36 us -> 37 us
    pallas_call x1, Pallas kernels: 30.3 us -> 31.3 us  [on_device_fused(): pl.pallas_call(functools.partial(fused_kernel, lon_count), out_shape=(jax...]
where the time goes in v3:
time: 37.9 us; the launch traced here: 37.7 us
  Pallas kernels  37 us (98%)
  between operations  0.64 us (2%)
    pallas_call x1, Pallas kernels, on_device_fused(): pl.pallas_call(functools.partial(fused_kernel, lon_count), out_shape=(jax...  31.3 us
    pallas_call x1, Pallas kernels, on_device_fused(): pl.pallas_call(gradient_kernel, grid=(local, halves), out_shape=(jax.Shap...  5.72 us

profile of v3, /device:TPU:0, one launch (start us, length us, event | category | flops | bytes accessed | tf_op | source)
XLA Modules:
  0.0 37.7 jit_solution(10956675623515815412)
XLA Ops:
  0.6 31.3 %shard_map.130 = (bf16[2,256,512]{2,1,0:T(8,128)(2,1)}, bf16[2,512,256]{2,1,0:T(8,128)(2,1)}, bf16[2,1024,512]{2,1,0:T(8,128)(2,1)}, bf16[2,512,1024]{2,1,0:T(8,...) custom-call(bf16[128,256]{1,0:T(8,128)(2,1)} %bitcast.11, ...), custom_call_target="tpu_custom_call" | custom-call | tf_op jit(solution)/shard_map/pallas_call | solution.py:700
  32.0 5.7 %shard_map.131 = (bf16[128,256]{1,0:T(8,128)(2,1)}, f32[256,2048]{1,0:T(8,128)}, f32[2048,256]{1,0:T(8,128)}) custom-call(bf16[2,256,512]{2,1,0:T(8,128)(2,1)} %get-tuple-element.13.x_ref, bf16[2,512,256]{2,1,0:T(8,128)(2,1)} %get-tuple-element.14.c_ref, bf16[2,1024,512]{2,1,0:T(8,128)(2,1)} %get-tuple-element.15.active_ref, ...), custom_call_target="tpu_custom_call" | custom-call | tf_op jit(solution)/shard_map/pallas_call | solution.py:756

commit v4 on v3

--- a/solution.py
+++ b/solution.py
@@ -237,6 +237,7 @@
 MESH = pl.DeviceIdType.MESH
 HALO = 32
 LANES = 128
+LAND = 1024.0
 
 
 def dot(left, right, dims=((1,), (0,))):
@@ -306,10 +307,10 @@
     kept_out,
     pick_out,
     store_sem,
-    ext,
-    keys,
-    vals,
-    flags,
+    sent,
+    ends,
+    sides,
+    window_data,
     qexp,
     own_kv,
     attended,
@@ -410,8 +411,14 @@
     loads[2].wait()
     loads[3].wait()
     state = state_ref[...].astype(f32)
-    ext[1, HALO : HALO + cells, :feats] = state_ref[...]
-    ext[1, HALO : HALO + cells, feats:] = jnp.broadcast_to(land_col, (cells, LANES)).astype(bf16)
+    shown = jnp.where(land_col > 0.5, state, LAND).astype(bf16)
+    sent[:cells] = shown
+    side_rows = cells // 2
+    side_id = iota((2 * side_rows, cells), 0)
+    low = lax.rem(side_id, side_rows)
+    wanted = low // 4 * 8 + lax.rem(low, 4) + jnp.where(side_id < side_rows, 0, 4)
+    to_sides = (wanted == iota((2 * side_rows, cells), 1)).astype(bf16)
+    sent[cells:] = dot(to_sides, shown).astype(bf16)
     tangent = (cot_ref[...].astype(f32) * land_col).astype(bf16)
     send_c[...] = dot(to_slots, tangent).astype(bf16).reshape(lon_count, slots, feats)
     got_c[0, pl.ds(lon, 1)] = send_c[pl.ds(lon, 1)]
@@ -420,15 +427,22 @@
 
     halo_copies = []
     for index, (dlat, dlon) in enumerate(near):
+        edge = HALO if dlon == 0 else HALO // 2
+        body = cells if dlon == 0 else side_rows
+        first = {0: 0, -1: cells, 1: cells + side_rows}[dlon]
         if dlat == 0:
-            src, dst = (HALO, cells), (HALO, cells)
+            src, dst = (first, body), (edge, body)
         elif dlat == 1:
-            src, dst = (cells, HALO), (0, HALO)
+            src, dst = (first + body - edge, edge), (0, edge)
         else:
-            src, dst = (HALO, HALO), (HALO + cells, HALO)
+            src, dst = (first, edge), (edge + body, edge)
+        if dlon == 0:
+            target = ends.at[pl.ds(0 if dlat == 1 else edge, edge)]
+        else:
+            target = sides.at[0 if dlon == -1 else 1, pl.ds(*dst)]
         copy = remote(
-            ext.at[1, pl.ds(*src)],
-            ext.at[1 - dlon, pl.ds(*dst)],
+            sent.at[pl.ds(*src)],
+            target,
             halo_send.at[index],
             halo_recv.at[index],
             shifted(dlat, dlon),
@@ -485,40 +499,37 @@
     centre = jnp.concatenate(centre_rows, axis=0)
     head_rows = jnp.concatenate([head_mask] * 8, axis=0)
 
+    total_rows = 2 * (cells + 2 * HALO)
+    window_id = iota((total_rows, 1), 0)
+    ext_lat, ext_col = window_id // 16, lax.rem(window_id, 16)
+    edge_lat = HALO // 8
+    end_at = jnp.where(ext_lat < edge_lat, ext_lat, ext_lat - rows)
+    in_end = jnp.logical_or(ext_lat < edge_lat, ext_lat >= edge_lat + rows)
+    middle_at = jnp.where(in_end, end_at * 8, 2 * HALO + (ext_lat - edge_lat) * 8) + ext_col
+    side_at = 2 * HALO + cells + ext_lat * 4 + lax.rem(ext_col, 4)
+    side_at = side_at + jnp.where(ext_col < 12, 0, total_rows // 4)
+    source_row = jnp.where(ext_col < 8, middle_at, side_at)
+    low_lat = jnp.where(lat == 0, edge_lat, 0)
+    high_lat = jnp.where(lat == 3, edge_lat + rows, 2 * edge_lat + rows)
+    on_grid = jnp.logical_and(ext_lat >= low_lat, ext_lat < high_lat)
+    source_row = jnp.where(on_grid, source_row, -1)
+    placing = (iota((total_rows, total_rows), 1) == source_row).astype(bf16)
+
     for copy in halo_copies:
         copy.wait()
 
     ext_rows = cells + 2 * HALO
-    from_right = lax.rem(iota((ext_rows, 1), 0), 8) < reach
-    around = jnp.where(from_right, ext[2].astype(f32), ext[0].astype(f32))
-    middle = ext[1].astype(f32)
-    ends = jnp.concatenate([middle[:HALO], middle[HALO + cells :]], axis=0)
-
-    def interleave(own, other):
-        groups = ext_rows // 8
-        width = own.shape[1]
-        both = jnp.concatenate(
-            [own.reshape(groups, 8, width), other.reshape(groups, 8, width)], axis=1
-        )
-        return both.reshape(2 * ext_rows, width)
-
-    normed_far = jnp.concatenate(
-        [norm_rows(ends[:, :feats], gain1_ref[...]), norm_rows(around[:, :feats], gain1_ref[...])],
-        axis=0,
-    )
-    for target, start in ((keys, 0), (vals, feats)):
-        far_part = dot(normed_far, proj_ref[:, feats + start : 2 * feats + start])
-        own = jnp.concatenate(
-            [far_part[:HALO], own_kv[:, start : start + feats], far_part[HALO : 2 * HALO]], axis=0
-        )
-        target[...] = interleave(own, far_part[2 * HALO :]).astype(bf16)
-    ext_lat = iota((2 * ext_rows, 1), 0) // 16
-    low = jnp.where(lat == 0, HALO // 8, 0)
-    high = jnp.where(lat == 3, (HALO + cells) // 8, ext_rows // 8)
-    on_grid = jnp.logical_and(ext_lat >= low, ext_lat < high)
-    flags[...] = jnp.where(on_grid, interleave(middle[:, feats:], around[:, feats:]), 0.0).astype(
-        bf16
-    )
+    far = jnp.concatenate([ends[...], sides[0], sides[1]], axis=0).astype(f32)
+    far_kv = dot(norm_rows(far, gain1_ref[...]), proj_ref[:, feats:])
+    ocean_far = (far[:, :LANES] < 0.5 * LAND).astype(f32)
+    ocean_own = jnp.broadcast_to(land_col, (cells, LANES))
+
+    def in_order(end, own, side):
+        return dot(placing, jnp.concatenate([end, own, side], axis=0).astype(bf16)).astype(bf16)
+
+    two = 2 * HALO
+    window_data[:, : 2 * feats] = in_order(far_kv[:two], own_kv[...], far_kv[two:])
+    window_data[:, 2 * feats :] = in_order(ocean_far[:two], ocean_own, ocean_far[two:])
 
     for copy in c_copies:
         copy.wait()
@@ -539,15 +550,15 @@
         rows_q = qexp[rows_of, :]
         parts = []
         for k, window in enumerate(windows):
-            ocean = dot(ones, flags[window, :], ((1,), (1,)))[:1]
-            raw = dot(rows_q[k * per_row : (k + 1) * per_row], keys[window, :], ((1,), (1,)))
+            ocean = dot(ones, window_data[window, 2 * feats :], ((1,), (1,)))[:1]
+            raw = dot(rows_q[k * per_row : (k + 1) * per_row], window_data[window, :feats], ((1,), (1,)))
             valid = jnp.where(ocean > 0.5, inside, centre) > 0.5
             parts.append(jnp.where(valid, raw * scale + bias, -jnp.inf))
         raw = jnp.concatenate(parts, axis=0)
         powers = jnp.exp(raw - jnp.max(raw, axis=1, keepdims=True))
         weights = (powers / jnp.sum(powers, axis=1, keepdims=True)).astype(bf16)
         for k, window in enumerate(windows):
-            mixed = dot(weights[k * per_row : (k + 1) * per_row], vals[window, :]) * head_rows
+            mixed = dot(weights[k * per_row : (k + 1) * per_row], window_data[window, feats : 2 * feats]) * head_rows
             mixed = jnp.sum(mixed.reshape(8, heads, feats), axis=1)
             attended[pl.ds(pl.multiple_of((i * batch + k) * 8, 8), 8), :] = mixed
         return carry
@@ -601,7 +612,7 @@
             x_rows = got_x[band, :, e * 16 : (e + 1) * 16, :].reshape(count, feats)
             c_rows = got_c[band, :, e * 16 : (e + 1) * 16, :].reshape(count, feats)
             here = slice(band * count, (band + 1) * count)
-            x_out[e, :, here] = x_rows.T
+            x_out[e, here, :] = x_rows
             c_out[e, here, :] = c_rows
             total = jnp.zeros((count, feats), f32)
             for start in range(e * units, (e + 1) * units, feats):
@@ -610,13 +621,13 @@
                 act, slope = gelu_parts(dot(x_rows, up_ref[:, part]))
                 act = act.astype(bf16)
                 back = dot(c_rows, down_ref[part, :], ((1,), (1,)))
-                active[e, spot, here] = act.T
+                active[e, here, spot] = act
                 pre_act[e, here, spot] = (back * slope).astype(bf16)
                 if band == 0:
                     total += dot(act, down_ref[part, :])
-            store(x_out.at[e, :, here], x_hbm.at[e, :, here])
+            store(x_out.at[e, here], x_hbm.at[e, here])
             store(c_out.at[e, here], c_hbm.at[e, here])
-            store(active.at[e, :, here], active_hbm.at[e, :, here])
+            store(active.at[e, here], active_hbm.at[e, here])
             store(pre_act.at[e, here], pre_hbm.at[e, here])
             if band == 0:
                 made.append(total.astype(bf16))
@@ -655,8 +666,8 @@
     block_ref[...] = (kept_ref[...].astype(jnp.float32) + dot(pick_ref[...], returned_ref[...])).astype(
         jnp.bfloat16
     )
-    gup_ref[...] = dot(x_ref[0], pre_ref[0])
-    gdown_ref[...] = dot(active_ref[0], c_ref[0])
+    gup_ref[...] = dot(x_ref[0], pre_ref[0], ((0,), (0,)))
+    gdown_ref[...] = dot(active_ref[0], c_ref[0], ((0,), (0,)))
 
 
 def on_device_fused(
@@ -700,9 +711,9 @@
     made = pl.pallas_call(
         functools.partial(fused_kernel, lon_count),
         out_shape=(
-            jax.ShapeDtypeStruct((local, feats, all_rows), bf16),
             jax.ShapeDtypeStruct((local, all_rows, feats), bf16),
-            jax.ShapeDtypeStruct((local, units, all_rows), bf16),
+            jax.ShapeDtypeStruct((local, all_rows, feats), bf16),
+            jax.ShapeDtypeStruct((local, all_rows, units), bf16),
             jax.ShapeDtypeStruct((local, all_rows, units), bf16),
             jax.ShapeDtypeStruct((cells, feats), bf16),
             jax.ShapeDtypeStruct((cells, EXPERTS * 16), bf16),
@@ -713,17 +724,17 @@
         scratch_shapes=[
             *(pltpu.VMEM(operand.shape, operand.dtype) for operand in operands),
             dma((11,)),
-            pltpu.VMEM((local, feats, all_rows), bf16),
             pltpu.VMEM((local, all_rows, feats), bf16),
-            pltpu.VMEM((local, units, all_rows), bf16),
+            pltpu.VMEM((local, all_rows, feats), bf16),
+            pltpu.VMEM((local, all_rows, units), bf16),
             pltpu.VMEM((local, all_rows, units), bf16),
             pltpu.VMEM((cells, feats), bf16),
             pltpu.VMEM((cells, EXPERTS * 16), bf16),
             dma((3 + 16 * local,)),
-            pltpu.VMEM((3, ext_rows, feats + LANES), bf16),
-            pltpu.VMEM((2 * ext_rows, feats), bf16),
-            pltpu.VMEM((2 * ext_rows, feats), bf16),
-            pltpu.VMEM((2 * ext_rows, LANES), bf16),
+            pltpu.VMEM((2 * cells, feats), bf16),
+            pltpu.VMEM((2 * HALO, feats), bf16),
+            pltpu.VMEM((2, ext_rows // 2, feats), bf16),
+            pltpu.VMEM((2 * ext_rows, 2 * feats + LANES), bf16),
             pltpu.VMEM((cells * heads, feats), bf16),
             pltpu.VMEM((cells, 2 * feats), f32),
             pltpu.VMEM((cells, feats), f32),
@@ -762,9 +773,9 @@
             jax.ShapeDtypeStruct(down_weight.shape, f32),
         ),
         in_specs=[
-            pl.BlockSpec((1, feats, all_rows), lambda e, u: (e, 0, 0)),
             pl.BlockSpec((1, all_rows, feats), lambda e, u: (e, 0, 0)),
-            pl.BlockSpec((1, wide, all_rows), lambda e, u: (e, u, 0)),
+            pl.BlockSpec((1, all_rows, feats), lambda e, u: (e, 0, 0)),
+            pl.BlockSpec((1, all_rows, wide), lambda e, u: (e, 0, u)),
             pl.BlockSpec((1, all_rows, wide), lambda e, u: (e, 0, u)),
             pl.BlockSpec((cells, feats), lambda e, u: (0, 0)),
             pl.BlockSpec((cells, EXPERTS * 16), lambda e, u: (0, 0)),

time: 37.9 us -> 35.2 us (0.929)
  Pallas kernels: 37 us -> 34.4 us
    pallas_call x1, Pallas kernels: 31.3 us -> 28.7 us  [on_device_fused(): pl.pallas_call(functools.partial(fused_kernel, lon_count), out_shape=(jax...]
where the time goes in v4:
time: 35.2 us; the launch traced here: 35 us
  Pallas kernels  34.4 us (98%)
  between operations  0.64 us (2%)
    pallas_call x1, Pallas kernels, on_device_fused(): pl.pallas_call(functools.partial(fused_kernel, lon_count), out_shape=(jax...  28.7 us
    pallas_call x1, Pallas kernels, on_device_fused(): pl.pallas_call(gradient_kernel, grid=(local, halves), out_shape=(jax.Shap...  5.73 us

profile of v4, /device:TPU:0, one launch (start us, length us, event | category | flops | bytes accessed | tf_op | source)
XLA Modules:
  0.0 35.0 jit_solution(631321677438894761)
XLA Ops:
  0.6 28.7 %shard_map.130 = (bf16[2,512,256]{2,1,0:T(8,128)(2,1)}, bf16[2,512,256]{2,1,0:T(8,128)(2,1)}, bf16[2,512,1024]{2,1,0:T(8,128)(2,1)}, bf16[2,512,1024]{2,1,0:T(8,...) custom-call(bf16[128,256]{1,0:T(8,128)(2,1)} %bitcast.11, ...), custom_call_target="tpu_custom_call" | custom-call | tf_op jit(solution)/shard_map/pallas_call | solution.py:711
  29.3 5.7 %shard_map.131 = (bf16[128,256]{1,0:T(8,128)(2,1)}, f32[256,2048]{1,0:T(8,128)}, f32[2048,256]{1,0:T(8,128)}) custom-call(bf16[2,512,256]{2,1,0:T(8,128)(2,1)} %get-tuple-element.13.x_ref, bf16[2,512,256]{2,1,0:T(8,128)(2,1)} %get-tuple-element.14.c_ref, bf16[2,512,1024]{2,1,0:T(8,128)(2,1)} %get-tuple-element.15.active_ref, ...), custom_call_target="tpu_custom_call" | custom-call | tf_op jit(solution)/shard_map/pallas_call | solution.py:767

commit v5 on v4

--- a/solution.py
+++ b/solution.py
@@ -300,8 +300,6 @@
     up_ref,
     down_ref,
     load_sem,
-    x_out,
-    c_out,
     active,
     pre_act,
     kept_out,
@@ -606,14 +604,18 @@
     store(kept_out, kept_hbm)
     store(pick_out, pick_hbm)
 
-    def experts_on(band):
+    def rows_out(band):
+        for e in range(local):
+            taken, here = pl.ds(e * 16, 16), pl.ds(band * lon_count, lon_count)
+            store(got_x.at[band, :, taken], x_hbm.at[e, here])
+            store(got_c.at[band, :, taken], c_hbm.at[e, here])
+
+    def experts_on(band, chosen):
         made = []
-        for e in range(local):
+        for e in chosen:
             x_rows = got_x[band, :, e * 16 : (e + 1) * 16, :].reshape(count, feats)
             c_rows = got_c[band, :, e * 16 : (e + 1) * 16, :].reshape(count, feats)
             here = slice(band * count, (band + 1) * count)
-            x_out[e, here, :] = x_rows
-            c_out[e, here, :] = c_rows
             total = jnp.zeros((count, feats), f32)
             for start in range(e * units, (e + 1) * units, feats):
                 part = slice(start, start + feats)
@@ -625,33 +627,34 @@
                 pre_act[e, here, spot] = (back * slope).astype(bf16)
                 if band == 0:
                     total += dot(act, down_ref[part, :])
-            store(x_out.at[e, here], x_hbm.at[e, here])
-            store(c_out.at[e, here], c_hbm.at[e, here])
             store(active.at[e, here], active_hbm.at[e, here])
             store(pre_act.at[e, here], pre_hbm.at[e, here])
             if band == 0:
                 made.append(total.astype(bf16))
         return made
 
-    for e, made in enumerate(experts_on(0)):
+    c_far.wait()
+    c_diag = remote(got_c.at[2], got_c.at[3], lat_send.at[3], lat_recv.at[3], (core_mate, lon))
+    c_diag.start()
+    for e, made in enumerate(experts_on(0, range(local))):
         send_o[:, e * 16 : (e + 1) * 16, :] = made.reshape(lon_count, 16, feats)
     o_copies = to_peers(send_o, got_o, o_send, o_recv)
     got_o[pl.ds(lon, 1)] = send_o[pl.ds(lon, 1)]
-
-    c_far.wait()
-    c_diag = remote(got_c.at[2], got_c.at[3], lat_send.at[3], lat_recv.at[3], (core_mate, lon))
-    c_diag.start()
+    rows_out(0)
+
     c_core.wait()
     x_core.wait()
-    experts_on(1)
+    rows_out(1)
+    experts_on(1, range(local // 2))
     for copy in far:
         copy.wait()
     x_diag = remote(got_x.at[2], got_x.at[3], lat_send.at[4], lat_recv.at[4], (core_mate, lon))
     x_diag.start()
-    experts_on(2)
+    rows_out(2)
+    experts_on(1, range(local // 2, local))
     c_diag.wait()
     x_diag.wait()
-    experts_on(3)
+    rows_out(3)
 
     for copy in o_copies:
         copy.wait()
@@ -661,13 +664,34 @@
 
 
 def gradient_kernel(
-    x_ref, c_ref, active_ref, pre_ref, kept_ref, pick_ref, returned_ref, block_ref, gup_ref, gdown_ref
+    x_ref,
+    c_ref,
+    active_ref,
+    pre_ref,
+    kept_ref,
+    pick_ref,
+    returned_ref,
+    up_ref,
+    down_ref,
+    block_ref,
+    gup_ref,
+    gdown_ref,
+    x_turned,
 ):
-    block_ref[...] = (kept_ref[...].astype(jnp.float32) + dot(pick_ref[...], returned_ref[...])).astype(
-        jnp.bfloat16
-    )
-    gup_ref[...] = dot(x_ref[0], pre_ref[0], ((0,), (0,)))
-    gdown_ref[...] = dot(active_ref[0], c_ref[0], ((0,), (0,)))
+    done = active_ref.shape[1]
+
+    @pl.when(pl.program_id(1) == 0)
+    def _():
+        x_turned[...] = x_ref[0].T
+        made = dot(pick_ref[...], returned_ref[...])
+        block_ref[...] = (kept_ref[...].astype(jnp.float32) + made).astype(jnp.bfloat16)
+
+    act, slope = gelu_parts(dot(x_ref[0, done:], up_ref[...]))
+    back = dot(c_ref[0, done:], down_ref[...], ((1,), (1,)))
+    pre_act = jnp.concatenate([pre_ref[0], (back * slope).astype(jnp.bfloat16)], axis=0)
+    active = jnp.concatenate([active_ref[0], act.astype(jnp.bfloat16)], axis=0)
+    gup_ref[...] = dot(x_turned[...], pre_act)
+    gdown_ref[...] = dot(active, c_ref[0], ((0,), (0,)))
 
 
 def on_device_fused(
@@ -711,10 +735,10 @@
     made = pl.pallas_call(
         functools.partial(fused_kernel, lon_count),
         out_shape=(
-            jax.ShapeDtypeStruct((local, all_rows, feats), bf16),
-            jax.ShapeDtypeStruct((local, all_rows, feats), bf16),
-            jax.ShapeDtypeStruct((local, all_rows, units), bf16),
-            jax.ShapeDtypeStruct((local, all_rows, units), bf16),
+            jax.ShapeDtypeStruct((local, 4 * lon_count, 16, feats), bf16),
+            jax.ShapeDtypeStruct((local, 4 * lon_count, 16, feats), bf16),
+            jax.ShapeDtypeStruct((local, all_rows // 2, units), bf16),
+            jax.ShapeDtypeStruct((local, all_rows // 2, units), bf16),
             jax.ShapeDtypeStruct((cells, feats), bf16),
             jax.ShapeDtypeStruct((cells, EXPERTS * 16), bf16),
             jax.ShapeDtypeStruct((lon_count, slots, feats), bf16),
@@ -724,13 +748,11 @@
         scratch_shapes=[
             *(pltpu.VMEM(operand.shape, operand.dtype) for operand in operands),
             dma((11,)),
-            pltpu.VMEM((local, all_rows, feats), bf16),
-            pltpu.VMEM((local, all_rows, feats), bf16),
-            pltpu.VMEM((local, all_rows, units), bf16),
-            pltpu.VMEM((local, all_rows, units), bf16),
+            pltpu.VMEM((local, all_rows // 2, units), bf16),
+            pltpu.VMEM((local, all_rows // 2, units), bf16),
             pltpu.VMEM((cells, feats), bf16),
             pltpu.VMEM((cells, EXPERTS * 16), bf16),
-            dma((3 + 16 * local,)),
+            dma((3 + 12 * local,)),
             pltpu.VMEM((2 * cells, feats), bf16),
             pltpu.VMEM((2 * HALO, feats), bf16),
             pltpu.VMEM((2, ext_rows // 2, feats), bf16),
@@ -762,7 +784,7 @@
             collective_id=0, has_side_effects=True, vmem_limit_bytes=56 * 1024 * 1024
         ),
     )(*operands)
-    wide = units // 2
+    wide = feats
     halves = units // wide
     block, grad_up, grad_down = pl.pallas_call(
         gradient_kernel,
@@ -775,19 +797,28 @@
         in_specs=[
             pl.BlockSpec((1, all_rows, feats), lambda e, u: (e, 0, 0)),
             pl.BlockSpec((1, all_rows, feats), lambda e, u: (e, 0, 0)),
-            pl.BlockSpec((1, all_rows, wide), lambda e, u: (e, 0, u)),
-            pl.BlockSpec((1, all_rows, wide), lambda e, u: (e, 0, u)),
+            pl.BlockSpec((1, all_rows // 2, wide), lambda e, u: (e, 0, u)),
+            pl.BlockSpec((1, all_rows // 2, wide), lambda e, u: (e, 0, u)),
             pl.BlockSpec((cells, feats), lambda e, u: (0, 0)),
             pl.BlockSpec((cells, EXPERTS * 16), lambda e, u: (0, 0)),
             pl.BlockSpec((EXPERTS * 16, feats), lambda e, u: (0, 0)),
+            pl.BlockSpec((feats, wide), lambda e, u: (0, e * halves + u)),
+            pl.BlockSpec((wide, feats), lambda e, u: (e * halves + u, 0)),
         ],
         out_specs=(
             pl.BlockSpec((cells, feats), lambda e, u: (0, 0)),
             pl.BlockSpec((feats, wide), lambda e, u: (0, e * halves + u)),
             pl.BlockSpec((wide, feats), lambda e, u: (e * halves + u, 0)),
         ),
+        scratch_shapes=[pltpu.VMEM((feats, all_rows), bf16)],
         compiler_params=pltpu.CompilerParams(vmem_limit_bytes=56 * 1024 * 1024),
-    )(*made[:6], made[6].reshape(EXPERTS * 16, feats))
+    )(
+        *(rows.reshape(local, all_rows, feats) for rows in made[:2]),
+        *made[2:6],
+        made[6].reshape(EXPERTS * 16, feats),
+        up_weight,
+        down_weight,
+    )
     return (block.reshape(lat_rows, lon_cols, feats), grad_up, grad_down)
 
 

time: 35.2 us -> 39.1 us (1.11)
  Pallas kernels: 34.4 us -> 38.1 us
    pallas_call x1, Pallas kernels: 5.73 us -> 9.8 us  [on_device_fused(): pl.pallas_call(gradient_kernel, grid=(local, halves), out_shape=(jax.Shap...]
where the time goes in v5:
time: 39.1 us; the launch traced here: 38.8 us
  Pallas kernels  38.1 us (97%)
  between operations  0.64 us (2%)
    pallas_call x1, Pallas kernels, on_device_fused(): pl.pallas_call(functools.partial(fused_kernel, lon_count), out_shape=(jax...  28.3 us
    pallas_call x1, Pallas kernels, on_device_fused(): pl.pallas_call(gradient_kernel, grid=(local, halves), out_shape=(jax.Shap...  9.8 us

profile of v5, /device:TPU:0, one launch (start us, length us, event | category | flops | bytes accessed | tf_op | source)
XLA Modules:
  0.0 38.8 jit_solution(5428158415676638411)
XLA Ops:
  0.6 28.3 %shard_map.130 = (bf16[2,32,16,256]{3,2,1,0:T(8,128)(2,1)}, bf16[2,32,16,256]{3,2,1,0:T(8,128)(2,1)}, bf16[2,256,1024]{2,1,0:T(8,128)(2,1)}, bf16[2,256,1024]{2,...) custom-call(bf16[128,256]{1,0:T(8,128)(2,1)} %bitcast.15, ...), custom_call_target="tpu_custom_call" | custom-call | tf_op jit(solution)/shard_map/pallas_call | solution.py:735
  29.0 9.8 %shard_map.131 = (bf16[128,256]{1,0:T(8,128)(2,1)}, f32[256,2048]{1,0:T(8,128)}, f32[2048,256]{1,0:T(8,128)}) custom-call(bf16[2,512,256]{2,1,0:T(8,128)(2,1)} %bitcast.12, bf16[2,512,256]{2,1,0:T(8,128)(2,1)} %bitcast.13, bf16[2,256,1024]{2,1,0:T(8,128)(2,1)} %get-tuple-element.15.active_ref, bf16[2,256,1024]{2,1,0:T(8,128)(2,1)} %get-tuple-element.16.pre_ref, ...), custom_call_target="tpu_custom_call" | custom-call | tf_op jit(solution)/shard_map/pallas_call | solution.py:789

commit v6 on v4

--- a/solution.py
+++ b/solution.py
@@ -300,8 +300,6 @@
     up_ref,
     down_ref,
     load_sem,
-    x_out,
-    c_out,
     active,
     pre_act,
     kept_out,
@@ -331,15 +329,12 @@
     o_recv,
     lat_send,
     lat_recv,
-    fwd_send,
-    fwd_recv,
 ):
     cells, feats = state_ref.shape
     rows = land_ref.shape[1]
     heads = bias_ref.shape[0]
     head_dim = feats // heads
     local = EXPERTS // lon_count
-    slots = local * 16
     units = up_ref.shape[1] // local
     reach = WINDOW // 2
     f32, bf16 = jnp.float32, jnp.bfloat16
@@ -402,8 +397,13 @@
     same = (label_col == label_row).astype(f32)
     rank_row = jnp.sum(jnp.where(row_id < col_id, same, 0.0), axis=0, keepdims=True)
     rank_col = jnp.sum(jnp.where(col_id < row_id, same, 0.0), axis=1, keepdims=True)
-    slot_row = (label_row * 16.0 + rank_row).astype(jnp.int32)
-    slot_col = (label_col * 16.0 + rank_col).astype(jnp.int32)
+
+    def slot_of(label, rank):
+        label = label.astype(jnp.int32)
+        place = lax.rem(label, local) * lon_count + lax.div(label, local)
+        return place * 16 + rank.astype(jnp.int32)
+
+    slot_row, slot_col = slot_of(label_row, rank_row), slot_of(label_col, rank_col)
     all_slots = EXPERTS * 16
     to_slots = (iota((all_slots, cells), 0) == slot_row).astype(bf16)
     to_cells = (iota((cells, all_slots), 1) == slot_col).astype(bf16)
@@ -420,8 +420,9 @@
     to_sides = (wanted == iota((2 * side_rows, cells), 1)).astype(bf16)
     sent[cells:] = dot(to_sides, shown).astype(bf16)
     tangent = (cot_ref[...].astype(f32) * land_col).astype(bf16)
-    send_c[...] = dot(to_slots, tangent).astype(bf16).reshape(lon_count, slots, feats)
-    got_c[0, pl.ds(lon, 1)] = send_c[pl.ds(lon, 1)]
+    send_c[...] = dot(to_slots, tangent).astype(bf16).reshape(local, lon_count, 16, feats)
+    for e in range(local):
+        got_c[e, pl.ds(lon, 1)] = send_c[e, pl.ds(lon, 1)]
 
     pl.semaphore_wait(barrier, len(met))
 
@@ -450,18 +451,26 @@
         copy.start()
         halo_copies.append(copy)
 
-    def to_peers(source, target, sent, received):
+    def to_peers(source, target, sent, received, first):
         copies = []
         for step in range(1, lon_count):
             device = shifted(0, step)
             copy = remote(
-                source.at[device[1]], target.at[lon], sent.at[step], received.at[step], device
+                source.at[device[1]],
+                target.at[lon],
+                sent.at[first + step],
+                received.at[first + step],
+                device,
             )
             copy.start()
             copies.append(copy)
         return copies
 
-    c_copies = to_peers(send_c, got_c.at[0], c_send, c_recv)
+    c_copies = []
+    for e in range(local):
+        c_copies += to_peers(
+            send_c.at[e], got_c.at[e], c_send, c_recv, e * lon_count
+        )
 
     for index in (4, 5, 6):
         loads[index].wait()
@@ -533,8 +542,8 @@
 
     for copy in c_copies:
         copy.wait()
-    c_core = remote(got_c.at[0], got_c.at[1], lat_send.at[0], lat_recv.at[0], (core_mate, lon))
-    c_far = remote(got_c.at[0], got_c.at[2], lat_send.at[1], lat_recv.at[1], (x_mate, lon))
+    c_core = remote(got_c.at[pl.ds(0 * local, local)], got_c.at[pl.ds(1 * local, local)], lat_send.at[0], lat_recv.at[0], (core_mate, lon))
+    c_far = remote(got_c.at[pl.ds(0 * local, local)], got_c.at[pl.ds(2 * local, local)], lat_send.at[1], lat_recv.at[1], (x_mate, lon))
     c_far.start()
     c_core.start()
 
@@ -544,9 +553,9 @@
 
     batch = 4
 
-    def attend(i, carry):
-        windows = [pl.ds(pl.multiple_of((i * batch + k) * 16, 16), LANES) for k in range(batch)]
-        rows_of = pl.ds(pl.multiple_of(i * batch * per_row, batch * per_row), batch * per_row)
+    def attend(i):
+        windows = [slice((i * batch + k) * 16, (i * batch + k) * 16 + LANES) for k in range(batch)]
+        rows_of = slice(i * batch * per_row, (i + 1) * batch * per_row)
         rows_q = qexp[rows_of, :]
         parts = []
         for k, window in enumerate(windows):
@@ -560,35 +569,24 @@
         for k, window in enumerate(windows):
             mixed = dot(weights[k * per_row : (k + 1) * per_row], window_data[window, feats : 2 * feats]) * head_rows
             mixed = jnp.sum(mixed.reshape(8, heads, feats), axis=1)
-            attended[pl.ds(pl.multiple_of((i * batch + k) * 8, 8), 8), :] = mixed
-        return carry
-
-    lax.fori_loop(0, rows // batch, attend, 0)
+            attended[(i * batch + k) * 8 : (i * batch + k + 1) * 8, :] = mixed
+
+    for i in range(rows // batch):
+        attend(i)
 
     loads[7].wait()
     loads[8].wait()
     residual = (state + dot(attended[...].astype(bf16), outw_ref[...])).astype(bf16).astype(f32)
     second = norm_rows(residual, gain2_ref[...])
-    send_x[...] = dot(to_slots, second).astype(bf16).reshape(lon_count, slots, feats)
-    x_copies = to_peers(send_x, got_x.at[0], x_send, x_recv)
-    got_x[0, pl.ds(lon, 1)] = send_x[pl.ds(lon, 1)]
-
-    far = []
-    for step in range(lon_count):
-        if step > 0:
-            x_copies[step - 1].wait()
-        source = shifted(0, -step)[1]
-        copy = remote(
-            got_x.at[0, source],
-            got_x.at[2, source],
-            fwd_send.at[step],
-            fwd_recv.at[step],
-            (x_mate, lon),
-        )
-        copy.start()
-        far.append(copy)
-    x_core = remote(got_x.at[0], got_x.at[1], lat_send.at[2], lat_recv.at[2], (core_mate, lon))
-    x_core.start()
+    send_x[...] = dot(to_slots, second).astype(bf16).reshape(local, lon_count, 16, feats)
+    x_copies = [
+        to_peers(
+            send_x.at[e], got_x.at[e], x_send, x_recv, e * lon_count
+        )
+        for e in range(local)
+    ]
+    for e in range(local):
+        got_x[e, pl.ds(lon, 1)] = send_x[e, pl.ds(lon, 1)]
 
     loads[9].wait()
     loads[10].wait()
@@ -606,52 +604,74 @@
     store(kept_out, kept_hbm)
     store(pick_out, pick_hbm)
 
-    def experts_on(band):
-        made = []
-        for e in range(local):
-            x_rows = got_x[band, :, e * 16 : (e + 1) * 16, :].reshape(count, feats)
-            c_rows = got_c[band, :, e * 16 : (e + 1) * 16, :].reshape(count, feats)
-            here = slice(band * count, (band + 1) * count)
-            x_out[e, here, :] = x_rows
-            c_out[e, here, :] = c_rows
-            total = jnp.zeros((count, feats), f32)
-            for start in range(e * units, (e + 1) * units, feats):
-                part = slice(start, start + feats)
-                spot = slice(start - e * units, start - e * units + feats)
-                act, slope = gelu_parts(dot(x_rows, up_ref[:, part]))
-                act = act.astype(bf16)
-                back = dot(c_rows, down_ref[part, :], ((1,), (1,)))
-                active[e, here, spot] = act
-                pre_act[e, here, spot] = (back * slope).astype(bf16)
-                if band == 0:
-                    total += dot(act, down_ref[part, :])
-            store(x_out.at[e, here], x_hbm.at[e, here])
-            store(c_out.at[e, here], c_hbm.at[e, here])
-            store(active.at[e, here], active_hbm.at[e, here])
-            store(pre_act.at[e, here], pre_hbm.at[e, here])
+    def band_copy(source, target, e, index, mate):
+        slot = 3 + 3 * e + index
+        return remote(
+            got_x.at[source * local + e],
+            got_x.at[target * local + e],
+            lat_send.at[slot],
+            lat_recv.at[slot],
+            (mate, lon),
+        )
+
+    def rows_out(band, e):
+        here = pl.ds(band * lon_count, lon_count)
+        store(got_x.at[band * local + e], x_hbm.at[e, here])
+        store(got_c.at[band * local + e], c_hbm.at[e, here])
+
+    def expert_on(band, e):
+        x_rows = got_x[band * local + e].reshape(count, feats)
+        c_rows = got_c[band * local + e].reshape(count, feats)
+        here = slice(band * count, (band + 1) * count)
+        total = jnp.zeros((count, feats), f32)
+        for start in range(e * units, (e + 1) * units, feats):
+            part = slice(start, start + feats)
+            spot = slice(start - e * units, start - e * units + feats)
+            act, slope = gelu_parts(dot(x_rows, up_ref[:, part]))
+            act = act.astype(bf16)
+            back = dot(c_rows, down_ref[part, :], ((1,), (1,)))
+            active[e, here, spot] = act
+            pre_act[e, here, spot] = (back * slope).astype(bf16)
             if band == 0:
-                made.append(total.astype(bf16))
-        return made
-
-    for e, made in enumerate(experts_on(0)):
-        send_o[:, e * 16 : (e + 1) * 16, :] = made.reshape(lon_count, 16, feats)
-    o_copies = to_peers(send_o, got_o, o_send, o_recv)
-    got_o[pl.ds(lon, 1)] = send_o[pl.ds(lon, 1)]
+                total += dot(act, down_ref[part, :])
+        store(active.at[e, here], active_hbm.at[e, here])
+        store(pre_act.at[e, here], pre_hbm.at[e, here])
+        return total.astype(bf16)
+
+    far, core, diag, o_copies = [], [], [], []
+    for e in range(local):
+        for copy in x_copies[e]:
+            copy.wait()
+        far.append(band_copy(0, 2, e, 0, x_mate))
+        core.append(band_copy(0, 1, e, 1, core_mate))
+        far[e].start()
+        core[e].start()
+        send_o[e] = expert_on(0, e).reshape(lon_count, 16, feats)
+        o_copies += to_peers(
+            send_o.at[e], got_o.at[e], o_send, o_recv, e * lon_count
+        )
+        got_o[e, pl.ds(lon, 1)] = send_o[e, pl.ds(lon, 1)]
+        rows_out(0, e)
 
     c_far.wait()
-    c_diag = remote(got_c.at[2], got_c.at[3], lat_send.at[3], lat_recv.at[3], (core_mate, lon))
+    c_diag = remote(got_c.at[pl.ds(2 * local, local)], got_c.at[pl.ds(3 * local, local)], lat_send.at[2], lat_recv.at[2], (core_mate, lon))
     c_diag.start()
     c_core.wait()
-    x_core.wait()
-    experts_on(1)
-    for copy in far:
-        copy.wait()
-    x_diag = remote(got_x.at[2], got_x.at[3], lat_send.at[4], lat_recv.at[4], (core_mate, lon))
-    x_diag.start()
-    experts_on(2)
+    for e in range(local):
+        far[e].wait()
+        diag.append(band_copy(2, 3, e, 2, core_mate))
+        diag[e].start()
+        core[e].wait()
+        rows_out(1, e)
+        expert_on(1, e)
+    for e in range(local):
+        rows_out(2, e)
+        expert_on(2, e)
     c_diag.wait()
-    x_diag.wait()
-    experts_on(3)
+    for e in range(local):
+        diag[e].wait()
+        rows_out(3, e)
+        expert_on(3, e)
 
     for copy in o_copies:
         copy.wait()
@@ -688,7 +708,6 @@
     heads = pos_bias.shape[0]
     lon_count = lax.axis_size("lon")
     local = EXPERTS // lon_count
-    slots = local * 16
     units = up_weight.shape[1] // local
     ext_rows = cells + 2 * HALO
     bf16, f32 = jnp.bfloat16, jnp.float32
@@ -711,21 +730,19 @@
     made = pl.pallas_call(
         functools.partial(fused_kernel, lon_count),
         out_shape=(
-            jax.ShapeDtypeStruct((local, all_rows, feats), bf16),
-            jax.ShapeDtypeStruct((local, all_rows, feats), bf16),
+            jax.ShapeDtypeStruct((local, 4 * lon_count, 16, feats), bf16),
+            jax.ShapeDtypeStruct((local, 4 * lon_count, 16, feats), bf16),
             jax.ShapeDtypeStruct((local, all_rows, units), bf16),
             jax.ShapeDtypeStruct((local, all_rows, units), bf16),
             jax.ShapeDtypeStruct((cells, feats), bf16),
             jax.ShapeDtypeStruct((cells, EXPERTS * 16), bf16),
-            jax.ShapeDtypeStruct((lon_count, slots, feats), bf16),
+            jax.ShapeDtypeStruct((local, lon_count, 16, feats), bf16),
         ),
         in_specs=[hbm] * 11,
         out_specs=(hbm,) * 7,
         scratch_shapes=[
             *(pltpu.VMEM(operand.shape, operand.dtype) for operand in operands),
             dma((11,)),
-            pltpu.VMEM((local, all_rows, feats), bf16),
-            pltpu.VMEM((local, all_rows, feats), bf16),
             pltpu.VMEM((local, all_rows, units), bf16),
             pltpu.VMEM((local, all_rows, units), bf16),
             pltpu.VMEM((cells, feats), bf16),
@@ -739,24 +756,22 @@
             pltpu.VMEM((cells, 2 * feats), f32),
             pltpu.VMEM((cells, feats), f32),
             pltpu.VMEM((heads, LANES), f32),
-            pltpu.VMEM((lon_count, slots, feats), bf16),
-            pltpu.VMEM((lon_count, slots, feats), bf16),
-            pltpu.VMEM((4, lon_count, slots, feats), bf16),
-            pltpu.VMEM((4, lon_count, slots, feats), bf16),
-            pltpu.VMEM((lon_count, slots, feats), bf16),
-            pltpu.VMEM((lon_count, slots, feats), bf16),
+            pltpu.VMEM((local, lon_count, 16, feats), bf16),
+            pltpu.VMEM((local, lon_count, 16, feats), bf16),
+            pltpu.VMEM((4 * local, lon_count, 16, feats), bf16),
+            pltpu.VMEM((4 * local, lon_count, 16, feats), bf16),
+            pltpu.VMEM((local, lon_count, 16, feats), bf16),
+            pltpu.VMEM((local, lon_count, 16, feats), bf16),
             dma((8,)),
             dma((8,)),
-            dma((lon_count,)),
-            dma((lon_count,)),
-            dma((lon_count,)),
-            dma((lon_count,)),
-            dma((lon_count,)),
-            dma((lon_count,)),
-            dma((5,)),
-            dma((5,)),
-            dma((lon_count,)),
-            dma((lon_count,)),
+            dma((local * lon_count,)),
+            dma((local * lon_count,)),
+            dma((local * lon_count,)),
+            dma((local * lon_count,)),
+            dma((local * lon_count,)),
+            dma((local * lon_count,)),
+            dma((3 + 3 * local,)),
+            dma((3 + 3 * local,)),
         ],
         compiler_params=pltpu.CompilerParams(
             collective_id=0, has_side_effects=True, vmem_limit_bytes=56 * 1024 * 1024
@@ -787,7 +802,11 @@
             pl.BlockSpec((wide, feats), lambda e, u: (e * halves + u, 0)),
         ),
         compiler_params=pltpu.CompilerParams(vmem_limit_bytes=56 * 1024 * 1024),
-    )(*made[:6], made[6].reshape(EXPERTS * 16, feats))
+    )(
+        *(rows.reshape(local, all_rows, feats) for rows in made[:2]),
+        *made[2:6],
+        made[6].reshape(EXPERTS * 16, feats),
+    )
     return (block.reshape(lat_rows, lon_cols, feats), grad_up, grad_down)
 
 

time: 35.2 us -> 36.1 us (1.026)
  Pallas kernels: 34.4 us -> 35.2 us
    pallas_call x1, Pallas kernels: 28.7 us -> 29.5 us  [on_device_fused(): pl.pallas_call(functools.partial(fused_kernel, lon_count), out_shape=(jax...]
where the time goes in v6:
time: 36.1 us; the launch traced here: 35.9 us
  Pallas kernels  35.2 us (98%)
  between operations  0.64 us (2%)
    pallas_call x1, Pallas kernels, on_device_fused(): pl.pallas_call(functools.partial(fused_kernel, lon_count), out_shape=(jax...  29.5 us
    pallas_call x1, Pallas kernels, on_device_fused(): pl.pallas_call(gradient_kernel, grid=(local, halves), out_shape=(jax.Shap...  5.73 us

profile of v6, /device:TPU:0, one launch (start us, length us, event | category | flops | bytes accessed | tf_op | source)
XLA Modules:
  0.0 35.9 jit_solution(11800111769015825368)
XLA Ops:
  0.6 29.5 %shard_map.130 = (bf16[2,32,16,256]{3,2,1,0:T(8,128)(2,1)}, bf16[2,32,16,256]{3,2,1,0:T(8,128)(2,1)}, bf16[2,512,1024]{2,1,0:T(8,128)(2,1)}, bf16[2,512,1024]{2,...) custom-call(bf16[128,256]{1,0:T(8,128)(2,1)} %bitcast.15, ...), custom_call_target="tpu_custom_call" | custom-call | tf_op jit(solution)/shard_map/pallas_call | solution.py:730
  30.2 5.7 %shard_map.131 = (bf16[128,256]{1,0:T(8,128)(2,1)}, f32[256,2048]{1,0:T(8,128)}, f32[2048,256]{1,0:T(8,128)}) custom-call(bf16[2,512,256]{2,1,0:T(8,128)(2,1)} %bitcast.12, bf16[2,512,256]{2,1,0:T(8,128)(2,1)} %bitcast.13, bf16[2,512,1024]{2,1,0:T(8,128)(2,1)} %get-tuple-element.15.active_ref, bf16[2,512,1024]{2,1,0:T(8,128)(2,1)} %get-tuple-element.16.pre_ref, ...), custom_call_target="tpu_custom_call" | custom-call | tf_op jit(solution)/shard_map/pallas_call | solution.py:782
